TPU v7x, 32 devices: a whole 2x2x4 slice. The times are simulated.
32 devices in a mesh: groups: 2 (over y), chol: 4 (over z), walk: 2 (over x), orb: 2 (over core).
Axes of the slice: x: 2, y: 2, z: 4, core: 2. Of those that a mesh axis runs over, the one named last changes fastest.
Arguments:
- walkers: float32 [32, 2, 36864], P(('groups', 'walk'), None, ('chol', 'orb')), parts along dimension 0, may hold values from -6 to 6
- correlation_inverse: float32 [32, 2, 96, 96], P(('groups', 'walk')), parts along dimension 0, may hold values from -0.625 to 0.625
- half_vectors: bfloat16 [4096, 36864], P(('groups', 'walk'), ('chol', 'orb')), parts along dimension 0, may hold values from -0.01953125 to 0.01953125
- field_vectors: bfloat16 [4096, 384, 384], P(('groups', 'walk'), ('chol', 'orb')), parts along dimension 0, may hold values from -0.0048828125 to 0.0048828125
- samples: float32 [32, 2048], P('groups', 'walk'), parts along dimension 0, may hold values from -6 to 6
- source: int32 [32], P(('groups', 'walk')), parts along dimension 0, may hold values from 0 to 15
Outputs:
- walkers_next: float32 [32, 2, 36864], P(('groups', 'walk'), None, ('chol', 'orb')), parts along dimension 0
There are 2 independent parts, one for each index of `groups`. A program takes and returns all parts, laid end to end along the dimension named above; each array names one. Nothing has to cross between parts.
All inputs are finite; a program needn't handle non-finite values.
Results may differ from a plain program's by a relative error of at most 0.02.
Values may be sent and summed in bfloat16 or wider, within the bound.
A program may use at most 128 MiB of HBM per device.

v0:
```python
import jax
import jax.numpy as jnp
from jax import lax
from jax.sharding import PartitionSpec as P

TERMS = 4
NS_STEPS = 2


def for_sending(shard):
    return jax.tree.map(lambda a: a.astype(jnp.bfloat16) if a.dtype == jnp.float32 else a, shard)


def complex_product(left_real, left_imag, right_real, right_imag, formula):
    first = jnp.einsum(formula, left_real, right_real, precision=lax.Precision.HIGHEST)
    second = jnp.einsum(formula, left_imag, right_imag, precision=lax.Precision.HIGHEST)
    third = jnp.einsum(formula, left_real, right_imag, precision=lax.Precision.HIGHEST)
    fourth = jnp.einsum(formula, left_imag, right_real, precision=lax.Precision.HIGHEST)
    return (first - second, third + fourth)


def normalizer(gram_real, gram_imag):
    electrons = gram_real.shape[-1]
    identity = jnp.eye(electrons, dtype=jnp.float32)
    scale_factor = jnp.trace(gram_real, axis1=1, axis2=2) / electrons
    iter_real = gram_real / scale_factor[:, None, None]
    iter_imag = gram_imag / scale_factor[:, None, None]
    root_real = jnp.broadcast_to(identity, gram_real.shape)
    root_imag = jnp.zeros_like(gram_real)
    for sweep_index in range(NS_STEPS):
        prod_real, prod_imag = complex_product(
            root_real, root_imag, iter_real, iter_imag, "wij,wjk->wik"
        )
        step_real = 1.5 * identity - 0.5 * prod_real
        step_imag = -0.5 * prod_imag
        iter_real, iter_imag = complex_product(
            iter_real, iter_imag, step_real, step_imag, "wij,wjk->wik"
        )
        root_real, root_imag = complex_product(
            step_real, step_imag, root_real, root_imag, "wij,wjk->wik"
        )
    inverse_root = lax.rsqrt(scale_factor)[:, None, None]
    return (root_real * inverse_root, root_imag * inverse_root)


def field_apply(field_block, values):
    next_real = jnp.einsum(
        "wab,wbn->wan", field_block[:, 0], values[:, 0], preferred_element_type=jnp.float32
    )
    next_real = next_real - jnp.einsum(
        "wab,wbn->wan", field_block[:, 1], values[:, 1], preferred_element_type=jnp.float32
    )
    next_imag = jnp.einsum(
        "wab,wbn->wan", field_block[:, 0], values[:, 1], preferred_element_type=jnp.float32
    )
    next_imag = next_imag + jnp.einsum(
        "wab,wbn->wan", field_block[:, 1], values[:, 0], preferred_element_type=jnp.float32
    )
    return jnp.stack([next_real, next_imag], 1)


def body(walkers, correlation_inverse, half_vectors, field_vectors, samples, source):
    local_walkers = walkers.shape[0]
    row_block = field_vectors.shape[1]
    orbitals = field_vectors.shape[2]
    electrons = correlation_inverse.shape[2]
    grid = walkers.reshape(local_walkers, 2, row_block, electrons)
    theta_real, theta_imag = complex_product(
        grid[:, 0], grid[:, 1], correlation_inverse[:, 0], correlation_inverse[:, 1], "wmk,wkn->wmn"
    )
    theta = (
        jnp.stack([theta_real, theta_imag], 1)
        .reshape(local_walkers, 2, row_block * electrons)
        .astype(jnp.bfloat16)
    )
    all_theta = lax.all_gather(theta, "walk", axis=0, tiled=True)
    bias_part = jnp.einsum(
        "wcj,gj->wcg", all_theta, half_vectors, preferred_element_type=jnp.float32
    )
    bias = lax.psum(bias_part, ("chol", "orb"))
    coefficient = jnp.stack([bias[:, 1], samples - bias[:, 0]], 1).astype(jnp.bfloat16)
    field_part = jnp.einsum(
        "wcg,gab->wcab", coefficient, field_vectors, preferred_element_type=jnp.float32
    )
    field = lax.psum_scatter(field_part, "walk", scatter_dimension=0, tiled=True).astype(
        jnp.bfloat16
    )
    devices_rows = lax.axis_size(("chol", "orb"))
    sharers = devices_rows // local_walkers
    col_width = electrons // sharers
    parted = grid.reshape(local_walkers, 2, row_block, sharers, col_width)
    parted = parted.transpose(0, 3, 1, 2, 4).reshape(devices_rows, 2, row_block, col_width)
    columns = lax.all_to_all(
        parted.astype(jnp.bfloat16), ("chol", "orb"), split_axis=0, concat_axis=2, tiled=True
    ).astype(parted.dtype)
    spread = jnp.broadcast_to(field[:, None], (local_walkers, sharers, 2, row_block, orbitals))
    spread = spread.reshape(devices_rows, 2, row_block, orbitals)
    whole_field = lax.all_to_all(spread, ("chol", "orb"), split_axis=0, concat_axis=2, tiled=True)
    current = columns
    col_summed = columns
    for order_index in range(1, TERMS + 1):
        current = field_apply(whole_field, current.astype(jnp.bfloat16)) / order_index
        col_summed = col_summed + current
    returned = lax.all_to_all(
        col_summed.astype(jnp.bfloat16), ("chol", "orb"), split_axis=2, concat_axis=0, tiled=True
    ).astype(col_summed.dtype)
    returned = returned.reshape(local_walkers, sharers, 2, row_block, col_width)
    summed = returned.transpose(0, 2, 3, 1, 4).reshape(local_walkers, 2, row_block, electrons)
    whole = lax.all_gather(summed.astype(jnp.bfloat16), ("chol", "orb"), axis=2, tiled=True).astype(
        summed.dtype
    )
    gram_real, gram_imag = complex_product(
        whole[:, 0], -whole[:, 1], whole[:, 0], whole[:, 1], "wmi,wmj->wij"
    )
    gram_real = gram_real / orbitals
    gram_imag = gram_imag / orbitals
    root_real, root_imag = normalizer(gram_real, gram_imag)
    norm_real, norm_imag = complex_product(
        summed[:, 0], summed[:, 1], root_real, root_imag, "wmk,wkn->wmn"
    )
    normalized = jnp.stack([norm_real, norm_imag], 1).reshape(
        local_walkers, 2, row_block * electrons
    )
    moved = lax.all_gather(for_sending(normalized), "walk", axis=0, tiled=True).astype(
        normalized.dtype
    )
    return jnp.take(moved, source, axis=0)


def solution(mesh):
    placed = (
        P(("groups", "walk"), None, ("chol", "orb")),
        P(("groups", "walk"), None, None, None),
        P(("groups", "walk"), ("chol", "orb")),
        P(("groups", "walk"), ("chol", "orb"), None),
        P("groups", "walk"),
        P(("groups", "walk")),
    )
    return jax.shard_map(
        body,
        mesh=mesh,
        in_specs=placed,
        out_specs=P(("groups", "walk"), None, ("chol", "orb")),
        check_vma=False,
    )
```

profile of v0, /device:TPU:1, one launch (start us, length us, event | category | flops | bytes accessed | tf_op | source)
XLA Modules:
  0.0 239.7 jit_solution(14504771620466679729)
XLA Ops:
  6.5 1.1 copy.45
  7.8 0.5 fusion.37
  8.3 0.5 fusion.41
  8.7 0.5 fusion.29
  9.4 0.5 fusion.28
  10.0 6.3 %all_gather.9 = bf16[16,2,4608]{2,0,1:T(8,128)(2,1)S(1)} all-gather(bf16[8,2,4608]{2,0,1:T(8,128)(2,1)S(1)} %pad_maximum_fusion.1), channel_id=1, replica_groups=mesh['groups'=2,'chol'=4,'walk'=2,'orb'=2] {'walk'}, dimensions={0}, use_global_device_ids=true | all-gather | bytes 442368 | tf_op jit(solution)/shard_map/all_gather | solution.py:76
  16.3 7.2 %fusion.3 = f32[16,2,1024]{2,0,1:T(8,128)} fusion(bf16[16,2,4608]{2,0,1:T(8,128)(2,1)S(1)} %all_gather.9, bf16[1024,4608]{1,0:T(8,128)(2,1)} %param.8), kind=kOutput, calls=%fused_computation.4 | convolution fusion | flops 301989888 | bytes 9863168 | tf_op jit(solution)/shard_map/wcj,gj->wcg/dot_general | solution.py:77
  23.8 54.5 %all-reduce.2.cloned.1.call-done = f32[16,2,1024]{2,0,1:T(8,128)} async-done(((f32[16,2,1024]{2,0,1:T(8,128)}), f32[16,2,1024]{2,0,1:T(8,128)}) %all-reduce.2.cloned.1.call-update) | async-done | bytes 131088 | tf_op jit(solution)/shard_map/psum | solution.py:80
  78.3 0.8 slice.232
  79.1 0.8 fusion.78
  80.0 29.4 %fusion = f32[16,2,48,384]{3,0,2,1:T(8,128)} fusion(bf16[1024,48,384]{2,1,0:T(8,128)(2,1)} %param.9, bf16[16,1,1024]{2,0,1:T(8,128)(2,1)S(1)} %fusion.78, bf16[16,1,1024]{2,0,1:T(8,128)(2,1)S(1)} %slice.232), kind=kOutput, calls=%fused_computation.1 | convolution fusion | flops 1208090624 | bytes 40173568 | tf_op jit(solution)/shard_map/wcg,gab->wcab/dot_general | solution.py:82
  109.4 0.7 copy.46
  110.1 5.6 %all-to-all-start = ((bf16[8,2,48,96]{3,2,1,0:T(8,128)(2,1)}), bf16[8,2,48,96]{3,2,1,0:T(8,128)(2,1)S(1)}, u32[]{:S(2)}, u32[]{:S(2)}) async-start(bf16[8,2,48,96]{3,2,1,0:T(8,128)(2,1)} %copy.46), calls=%async_computation | async-start | bytes 393216 | tf_op jit(solution)/shard_map/all_to_all | solution.py:93
  115.7 29.1 %reduce-scatter.2.cloned.1.call-done = f32[8,2,48,384]{3,0,2,1:T(8,128)} async-done(((f32[16,2,48,384]{3,0,2,1:T(8,128)}), f32[8,2,48,384]{3,0,2,1:T(8,128)}) %reduce-scatter.2.cloned.1.call-update) | async-done | bytes 1179664 | tf_op jit(solution)/shard_map/reduce_scatter | solution.py:85
  144.9 1.3 convert_element_type.82
  146.2 0.9 copy.52
  147.1 5.3 %all-to-all-start.1 = ((bf16[8,2,48,384]{3,2,1,0:T(8,128)(2,1)}), bf16[8,2,48,384]{3,2,1,0:T(8,128)(2,1)S(1)}, u32[]{:S(2)}, u32[]{:S(2)}) async-start(bf16[8,2,48,384]{3,2,1,0:T(8,128)(2,1)} %copy.52), calls=%async_computation.2 | async-start | bytes 1179648 | tf_op jit(solution)/shard_map/all_to_all | solution.py:98
  152.6 15.7 %all-to-all-done.1 = bf16[8,2,48,384]{3,2,1,0:T(8,128)(2,1)S(1)} async-done(((bf16[8,2,48,384]{3,2,1,0:T(8,128)(2,1)}), bf16[8,2,48,384]{3,2,1,0:T(8,128)(2,1)S(1)}, u32[]{:S(2)}, u32[]{:S(2)}) %all-to-all-start.1) | async-done | bytes 589856 | tf_op jit(solution)/shard_map/all_to_all | solution.py:98
  168.4 0.3 fusion.65
  168.6 0.3 fusion.64
  168.9 0.3 fusion.26
  169.2 0.3 fusion.27
  169.7 0.2 fusion.72
  170.7 0.2 fusion.74
  170.9 0.2 fusion.22
  171.2 0.2 fusion.23
  171.9 0.2 fusion.20
  172.2 0.2 fusion.21
  172.7 9.7 %all_to_all.54 = bf16[1,2,384,96]{3,1,0,2:T(2,128)(2,1)S(1)} all-to-all(bf16[1,2,384,96]{3,1,0,2:T(2,128)(2,1)S(1)} %copy.54), channel_id=1, replica_groups=mesh['groups'=2,'chol'=4,'walk'=2,'orb'=2] {'chol','orb'}, dimensions={2} | all-to-all | bytes 294912 | tf_op jit(solution)/shard_map/all_to_all | solution.py:104
  182.4 0.7 copy.56
  183.3 24.6 %all-gather.3.cloned.1.call-done = bf16[8,1,2,384,96]{4,0,2,1,3:T(8,128)(2,1)} async-done(((bf16[8,1,2,48,96]{4,0,2,1,3:T(8,128)(2,1)}), bf16[8,1,2,384,96]{4,0,2,1,3:T(8,128)(2,1)}) %all-gather.3.cloned.1.call-update) | async-done | bytes 1179664 | tf_op jit(solution)/shard_map/all_gather | solution.py:109
  207.9 2.1 copy.57
  210.0 0.8 fusion.18
  210.8 0.8 fusion.16
  211.7 0.5 select_reduce_fusion
  212.2 0.4 fusion.7
  212.6 0.5 fusion.62
  213.1 0.5 fusion.58
  213.6 0.5 fusion.15
  214.1 0.5 fusion.60
  214.6 0.6 fusion.88
  215.2 0.5 fusion.52
  215.6 0.5 fusion.13
  216.2 0.6 fusion.87
  216.8 0.5 convolution_subtract_fusion.4
  217.2 0.5 convolution_subtract_fusion.3
  217.8 0.5 convolution_add_fusion.4
  218.3 0.5 convolution_add_fusion.3
  218.8 0.5 fusion.89
  219.3 0.5 fusion.91
  219.9 0.5 fusion.12
  220.4 0.5 fusion.92
  221.0 0.5 fusion.90
  221.5 0.5 fusion.10
  222.0 0.5 fusion.8
  222.6 0.8 fusion.9
  223.4 0.3 fusion.66
  223.7 0.3 fusion.67
  224.0 0.3 fusion.31
  224.5 0.3 fusion.30
  225.0 0.3 pad_maximum_fusion.2
  225.3 5.9 %all_gather.11 = bf16[16,2,4608]{2,1,0:T(2,128)(2,1)S(1)} all-gather(bf16[8,2,4608]{2,1,0:T(2,128)(2,1)S(1)} %pad_maximum_fusion.2), channel_id=1, replica_groups=mesh['groups'=2,'chol'=4,'walk'=2,'orb'=2] {'walk'}, dimensions={0}, use_global_device_ids=true | all-gather | bytes 442368 | tf_op jit(solution)/shard_map/all_gather | solution.py:124
  231.4 0.9 gather_fusion
  232.3 0.9 broadcast_select_fusion
  (43 shorter events, 3.4 us)
Async XLA Ops:
  6.5 1.3 copy-start
  6.5 71.8 %all-reduce.2.cloned.1.call-start = ((), (), s32[]{:S(2)}) async-start(), calls=%async_computation.4 | async-start | bytes 262144 | tf_op jit(solution)/shard_map/psum | solution.py:80
  16.3 62.8 %copy-start.1 = (f32[16,1024]{1,0:T(8,128)S(1)}, f32[16,1024]{1,0:T(8,128)}, u32[]{:S(2)}) copy-start(f32[16,1024]{1,0:T(8,128)} %param.10) | copy-start | bytes 196612
  23.5 121.3 %reduce-scatter.2.cloned.1.call-start = ((), (), s32[]{:S(2)}) async-start(), calls=%async_computation.5 | async-start | bytes 3538944 | tf_op jit(solution)/shard_map/reduce_scatter | solution.py:85
  110.1 37.0 %all-to-all-start = ((bf16[8,2,48,96]{3,2,1,0:T(8,128)(2,1)}), bf16[8,2,48,96]{3,2,1,0:T(8,128)(2,1)S(1)}, u32[]{:S(2)}, u32[]{:S(2)}) async-start(bf16[8,2,48,96]{3,2,1,0:T(8,128)(2,1)} %copy.46), calls=%async_computation | async-start | bytes 393216 | tf_op jit(solution)/shard_map/all_to_all | solution.py:93
  147.1 21.2 %all-to-all-start.1 = ((bf16[8,2,48,384]{3,2,1,0:T(8,128)(2,1)}), bf16[8,2,48,384]{3,2,1,0:T(8,128)(2,1)S(1)}, u32[]{:S(2)}, u32[]{:S(2)}) async-start(bf16[8,2,48,384]{3,2,1,0:T(8,128)(2,1)} %copy.52), calls=%async_computation.2 | async-start | bytes 1179648 | tf_op jit(solution)/shard_map/all_to_all | solution.py:98
  152.4 55.5 %all-gather.3.cloned.1.call-start = ((), (), s32[]{:S(2)}) async-start(), calls=%async_computation.6 | async-start | bytes 1769472 | tf_op jit(solution)/shard_map/all_gather | solution.py:109
  172.5 10.7 %copy-start.2 = (s32[8]{0:T(128)S(1)}, s32[8]{0:T(128)}, u32[]{:S(2)}) copy-start(s32[8]{0:T(128)} %param.11) | copy-start | bytes 100
Sparse Core Ops, SparseCore 0:
  23.7 54.5 all-reduce.1
  109.5 35.3 reduce-scatter.1
  183.3 24.5 all-gather.2
where the time goes:
time: 241 us; the launch traced here: 240 us
  waiting for transfers between devices  124 us (51%)
  matrix products  56.9 us (24%)
  blocking collectives  21.9 us (9%)
  between operations  13.5 us (6%)
  starting transfers between devices  11.1 us (5%)
  local copies, waits for them, and re-layouts  8.36 us (3%)
  other arithmetic  3.9 us (2%)
    psum x1, waiting for transfers between devices, body(): bias = lax.psum(bias_part, ('chol', 'orb'))  54.5 us
    dot_general x1, matrix products, body(): jnp.einsum('wcg,gab->wcab', coefficient, field_vectors, preferred_element...  29.4 us
    reduce_scatter x1, waiting for transfers between devices, body(): lax.psum_scatter(field_part, 'walk', scatter_dimension=0, tiled=True)  29.1 us
    all_gather x1, waiting for transfers between devices, body(): lax.all_gather(summed.astype(jnp.bfloat16), ('chol', 'orb'), axis=2, tile...  24.6 us
    all_to_all x1, waiting for transfers between devices, body(): lax.all_to_all(spread, ('chol', 'orb'), split_axis=0, concat_axis=2, tile...  15.7 us
    all_to_all x1, blocking collectives, body(): lax.all_to_all(col_summed.astype(jnp.bfloat16), ('chol', 'orb'), split_ax...  9.7 us
    dot_general x1, matrix products, body(): jnp.einsum('wcj,gj->wcg', all_theta, half_vectors, preferred_element_type...  7.21 us
    all_gather x1, blocking collectives, body(): all_theta = lax.all_gather(theta, 'walk', axis=0, tiled=True)  6.27 us
  transfers between devices with their start and end apart: 5, of which 4 were waited for; matrix products, arithmetic and copies ran while one was open for 1% of the time, Pallas kernels for 0%

commit v1 on v0

--- a/solution.py
+++ b/solution.py
@@ -1,6 +1,10 @@
+import functools
+
 import jax
 import jax.numpy as jnp
 from jax import lax
+from jax.experimental import pallas as pl
+from jax.experimental.pallas import tpu as pltpu
 from jax.sharding import PartitionSpec as P
 
 TERMS = 4
@@ -59,7 +63,7 @@
     return jnp.stack([next_real, next_imag], 1)
 
 
-def body(walkers, correlation_inverse, half_vectors, field_vectors, samples, source):
+def plain_body(walkers, correlation_inverse, half_vectors, field_vectors, samples, source):
     local_walkers = walkers.shape[0]
     row_block = field_vectors.shape[1]
     orbitals = field_vectors.shape[2]
@@ -127,6 +131,423 @@
     return jnp.take(moved, source, axis=0)
 
 
+MESH = pl.DeviceIdType.MESH
+LANES = 128
+HALF = 8
+ROWS = 16
+VECTORS = 64
+DEPTH = 4
+VMEM_LIMIT = 48 * 1024 * 1024
+
+
+def owner_id(index):
+    orbs = lax.axis_size("orb")
+    return {"chol": index // orbs, "orb": lax.rem(index, orbs)}
+
+
+def position():
+    return lax.axis_index("chol") * lax.axis_size("orb") + lax.axis_index("orb")
+
+
+def greet(devices):
+    barrier = pltpu.get_barrier_semaphore()
+    for device in devices:
+        pl.semaphore_signal(barrier, inc=1, device_id=device, device_id_type=MESH)
+    pl.semaphore_wait(barrier, len(devices))
+
+
+def cross(count, sharers):
+    me, walk = position(), lax.axis_index("walk")
+    rows = [owner_id(lax.rem(me + step, count)) for step in range(1, count)]
+    return rows + [{"walk": lax.rem(walk + step, sharers)} for step in range(1, sharers)]
+
+
+def remote(source, target, send, recv, device):
+    return pltpu.make_async_remote_copy(
+        src_ref=source, dst_ref=target, send_sem=send, recv_sem=recv,
+        device_id=device, device_id_type=MESH,
+    )
+
+
+def bias_kernel(count, sharers, theta_ref, half_ref, samples_ref, coef_ref,
+                half, theta, parts, arrived, load_sem, theta_send, theta_recv,
+                part_send, part_recv, coef_send, coef_recv):
+    me, walk = position(), lax.axis_index("walk")
+    width = half.shape[1]
+    local = theta_ref.shape[0] // 2
+
+    def load(index):
+        return pltpu.make_async_copy(
+            half_ref.at[pl.ds(pl.multiple_of(index * width, width), width), :],
+            half.at[index], load_sem.at[index],
+        )
+
+    def first(step, carry):
+        load(lax.rem(me + 1 + step, count)).start()
+        return carry
+
+    lax.fori_loop(0, count, first, 0)
+    greet(cross(count, sharers))
+    sends = []
+    for step in range(1, sharers):
+        other = lax.rem(walk + step, sharers)
+        sends.append(remote(theta_ref, theta.at[walk], theta_send.at[step],
+                            theta_recv.at[walk], {"walk": other}))
+        sends[-1].start()
+    theta[walk] = theta_ref[...]
+    for step in range(1, sharers):
+        other = lax.rem(walk + step, sharers)
+        remote(theta_ref, theta.at[other], theta_send.at[step],
+               theta_recv.at[other], {"walk": other}).wait_recv()
+
+    def product(index):
+        load(index).wait()
+        return lax.dot_general(
+            theta[...].reshape(sharers * 2 * local, theta.shape[2]), half[index],
+            (((1,), (1,)), ((), ())), preferred_element_type=jnp.float32,
+        )
+
+    def part_copy(index):
+        return remote(parts.at[index], arrived.at[me], part_send.at[index],
+                      part_recv.at[me], owner_id(index))
+
+    def one(step, carry):
+        index = lax.rem(me + 1 + step, count)
+        parts[index] = product(index)
+        part_copy(index).start()
+        return carry
+
+    lax.fori_loop(0, count - 1, one, 0)
+    arrived[me] = product(me)
+
+    def take(step, carry):
+        index = lax.rem(me + 1 + step, count)
+        remote(parts.at[index], arrived.at[index], part_send.at[index],
+               part_recv.at[index], owner_id(index)).wait_recv()
+        return carry
+
+    lax.fori_loop(0, count - 1, take, 0)
+    bias = jnp.sum(arrived[...], axis=0).reshape(sharers, 2, local, width)
+    chosen = samples_ref[:, pl.ds(pl.multiple_of(me * width, width), width)]
+    chosen = chosen.reshape(sharers, local, width)
+    pair = jnp.stack([bias[:, 1], chosen - bias[:, 0]], 1)
+    coef_ref[me] = pair.reshape(sharers * 2 * local, width).astype(jnp.bfloat16)
+
+    def spread(step, carry):
+        index = lax.rem(me + 1 + step, count)
+        remote(coef_ref.at[me], coef_ref.at[me], coef_send.at[index],
+               coef_recv.at[me], owner_id(index)).start()
+        return carry
+
+    lax.fori_loop(0, count - 1, spread, 0)
+
+    def finish(step, carry):
+        index = lax.rem(me + 1 + step, count)
+        part_copy(index).wait_send()
+        remote(coef_ref.at[me], coef_ref.at[index], coef_send.at[index],
+               coef_recv.at[index], owner_id(index)).wait()
+        return carry
+
+    lax.fori_loop(0, count - 1, finish, 0)
+    for send in sends:
+        send.wait_send()
+
+
+def field_kernel(count, sharers, coef_ref, columns_ref, vectors_ref, field_ref, whole_ref,
+                 spread, blocks, total, full, outgoing, incoming, finished,
+                 load_sem, column_send, column_recv, walk_send, walk_recv,
+                 row_send, row_recv):
+    me, walk = position(), lax.axis_index("walk")
+    local = columns_ref.shape[0]
+    row_block = columns_ref.shape[1]
+    orbitals = vectors_ref.shape[2]
+    chunks = vectors_ref.shape[0] // VECTORS
+    groups = row_block // ROWS
+    lines = coef_ref.shape[1]
+    per_block = coef_ref.shape[2] // VECTORS
+    depth = VECTORS * HALF
+
+    def load(step):
+        group, chunk = step // chunks, lax.rem(step, chunks)
+        slot = lax.rem(step, DEPTH)
+        return pltpu.make_async_copy(
+            vectors_ref.at[pl.ds(pl.multiple_of(chunk * VECTORS, VECTORS), VECTORS),
+                           pl.ds(pl.multiple_of(group * ROWS, ROWS), ROWS), :],
+            blocks.at[slot], load_sem.at[slot],
+        )
+
+    for step in range(DEPTH - 1):
+        load(jnp.int32(step)).start()
+    greet(cross(count, sharers))
+    here = pl.ds(pl.multiple_of(me * row_block, ROWS), row_block)
+
+    def column_copy(index):
+        return remote(columns_ref.at[index], whole_ref.at[here, :], column_send.at[index],
+                      column_recv.at[me], owner_id(index))
+
+    def send_columns(step, carry):
+        column_copy(lax.rem(me + 1 + step, count)).start()
+        return carry
+
+    lax.fori_loop(0, count - 1, send_columns, 0)
+    whole_ref[here, :] = columns_ref[me]
+
+    vector_at = lax.broadcasted_iota(jnp.int32, (LANES, depth), 0)
+    place = lax.broadcasted_iota(jnp.int32, (LANES, depth), 1)
+    row_at = lax.broadcasted_iota(jnp.int32, (HALF, depth), 0)
+    row_place = lax.broadcasted_iota(jnp.int32, (HALF, depth), 1)
+    diagonal = (lax.rem(row_place, HALF) == row_at).astype(jnp.float32)
+
+    for part in range(per_block):
+        picks = (vector_at == place // HALF + part * VECTORS).astype(jnp.bfloat16)
+
+        def widen(block, carry):
+            repeated = jnp.dot(coef_ref[block], picks, preferred_element_type=jnp.float32)
+            wide = repeated[:, None, :] * diagonal[None]
+            spread[block * per_block + part] = wide.reshape(lines * HALF, depth).astype(
+                jnp.bfloat16
+            )
+            return carry
+
+        lax.fori_loop(0, coef_ref.shape[0], widen, 0)
+
+    def walk_copy(group, step, arriving):
+        other = lax.rem(walk + step, sharers) if not arriving else lax.rem(
+            walk + sharers - step, sharers)
+        return remote(outgoing.at[group, other], incoming.at[group, other if arriving else walk],
+                      walk_send.at[group, other], walk_recv.at[group, other if arriving else walk],
+                      {"walk": other})
+
+    def row_copy(group, index, arriving):
+        giver = index if arriving else me
+        at = pl.ds(pl.multiple_of(giver * row_block + group * ROWS, ROWS), ROWS)
+        return remote(finished.at[group, index], field_ref.at[:, at, :],
+                      row_send.at[group, index], row_recv.at[group, giver], owner_id(index))
+
+    def deliver(group):
+        result = full[group, walk]
+        for step in range(1, sharers):
+            walk_copy(group, step, True).wait_recv()
+            other = lax.rem(walk + sharers - step, sharers)
+            result = result + incoming[group, other].astype(jnp.float32)
+        finished[group] = result.astype(jnp.bfloat16)
+
+        def send_rows(step, carry):
+            row_copy(group, lax.rem(me + 1 + step, count), False).start()
+            return carry
+
+        lax.fori_loop(0, count - 1, send_rows, 0)
+        field_ref[:, pl.ds(pl.multiple_of(me * row_block + group * ROWS, ROWS), ROWS), :] = (
+            finished[group, me]
+        )
+
+    for group in range(groups):
+        total[...] = jnp.zeros_like(total)
+
+        def add(chunk, carry):
+            step = group * chunks + chunk
+
+            @pl.when(step + DEPTH - 1 < groups * chunks)
+            def _():
+                load(step + DEPTH - 1).start()
+
+            load(step).wait()
+            block = blocks[lax.rem(step, DEPTH)]
+            upper = block[:, :HALF, :].reshape(depth, orbitals)
+            lower = block[:, HALF:, :].reshape(depth, orbitals)
+            total[...] += jnp.dot(
+                spread[chunk], jnp.concatenate([upper, lower], axis=1),
+                preferred_element_type=jnp.float32,
+            )
+            return carry
+
+        lax.fori_loop(0, chunks, add, 0)
+        result = total[...].reshape(sharers, 2, local, HALF, 2 * orbitals)
+        result = jnp.concatenate([result[..., :orbitals], result[..., orbitals:]], axis=3)
+        for part in range(2):
+            full[group, :, :, part] = result[:, part]
+            outgoing[group, :, :, part] = result[:, part].astype(jnp.bfloat16)
+        for step in range(1, sharers):
+            walk_copy(group, step, False).start()
+        if group > 0:
+            deliver(group - 1)
+    deliver(groups - 1)
+
+    def finish(step, carry):
+        index = lax.rem(me + 1 + step, count)
+        column_copy(index).wait_send()
+        there = pl.ds(pl.multiple_of(index * row_block, ROWS), row_block)
+        remote(columns_ref.at[index], whole_ref.at[there, :], column_send.at[index],
+               column_recv.at[index], owner_id(index)).wait_recv()
+        for group in range(groups):
+            row_copy(group, index, False).wait_send()
+            row_copy(group, index, True).wait_recv()
+        return carry
+
+    lax.fori_loop(0, count - 1, finish, 0)
+    for group in range(groups):
+        for step in range(1, sharers):
+            walk_copy(group, step, False).wait_send()
+
+
+def exact(left, right, dims=(((1,), (0,)), ((), ()))):
+    return lax.dot_general(left, right, dims, precision=lax.Precision.HIGHEST,
+                           preferred_element_type=jnp.float32)
+
+
+def walker_kernel(count, sharers, electrons, field_ref, whole_ref, out_ref,
+                  send_sem, recv_sem, rows):
+    me, walk = position(), lax.axis_index("walk")
+    row_block = rows.shape[1]
+    orbitals = field_ref.shape[1]
+    others = []
+    for across in range(sharers):
+        for step in range(count):
+            if across + step > 0:
+                target = owner_id(lax.rem(me + step, count))
+                target["walk"] = lax.rem(walk + across, sharers)
+                others.append((across, step, target))
+    greet([target for _, _, target in others])
+
+    def swap(value, sign):
+        return jnp.concatenate([-sign * value[:, LANES:], sign * value[:, :LANES]], axis=1)
+
+    current = whole_ref[...].astype(jnp.float32)
+    summed = current
+    for order_index in range(1, TERMS + 1):
+        rounded = current.astype(jnp.bfloat16)
+        real = jnp.dot(field_ref[0], rounded, preferred_element_type=jnp.float32)
+        imag = jnp.dot(field_ref[1], rounded, preferred_element_type=jnp.float32)
+        current = (real + swap(imag, 1.0)) / order_index
+        summed = summed + current
+    squares = exact(summed, summed, (((0,), (0,)), ((), ()))) / orbitals
+    gram_real = squares[:LANES, :LANES] + squares[LANES:, LANES:]
+    gram_imag = squares[:LANES, LANES:] - squares[LANES:, :LANES]
+    size = 2 * LANES
+    identity = (
+        lax.broadcasted_iota(jnp.int32, (size, size), 0)
+        == lax.broadcasted_iota(jnp.int32, (size, size), 1)
+    ).astype(jnp.float32)
+    scale = jnp.sum(gram_real * identity[:LANES, :LANES]) / electrons
+    top = jnp.concatenate([gram_real, gram_imag], axis=1)
+    bottom = jnp.concatenate([-gram_imag, gram_real], axis=1)
+    iterate = jnp.concatenate([top, bottom], axis=0) / scale
+    step_of = 1.5 * identity - 0.5 * iterate
+    root = step_of
+    for sweep_index in range(1, NS_STEPS):
+        iterate = exact(iterate, step_of)
+        step_of = 1.5 * identity - 0.5 * exact(root, iterate)
+        root = exact(step_of, root)
+    normalized = exact(summed, root * lax.rsqrt(scale))
+    rows[...] = normalized.reshape(count, row_block, size).astype(jnp.bfloat16)
+
+    mine = walk * count + me
+    for across, step, target in others:
+        index = lax.rem(me + step, count)
+        remote(rows.at[index], out_ref.at[mine], send_sem.at[across, step],
+               recv_sem.at[across, step], target).start()
+    out_ref[mine] = rows[me]
+    for across, step, target in others:
+        index = lax.rem(me + step, count)
+        giver = lax.rem(walk + sharers - across, sharers) * count + lax.rem(
+            me + count - step, count)
+        remote(rows.at[index], out_ref.at[giver], send_sem.at[across, step],
+               recv_sem.at[across, step], target).wait()
+
+
+def call(kernel, ident, shapes, places, scratch):
+    single = isinstance(shapes, jax.ShapeDtypeStruct)
+    spec = pl.BlockSpec(memory_space=pltpu.VMEM)
+    return pl.pallas_call(
+        kernel,
+        out_shape=shapes,
+        in_specs=[pl.BlockSpec(memory_space=place) for place in places],
+        out_specs=spec if single else [spec] * len(shapes),
+        scratch_shapes=scratch,
+        compiler_params=pltpu.CompilerParams(
+            collective_id=ident, has_side_effects=True, vmem_limit_bytes=VMEM_LIMIT
+        ),
+    )
+
+
+def body(walkers, correlation_inverse, half_vectors, field_vectors, samples, source):
+    local_walkers = walkers.shape[0]
+    vectors, row_block, orbitals = field_vectors.shape
+    electrons = correlation_inverse.shape[2]
+    flat = row_block * electrons
+    count = lax.axis_size(("chol", "orb"))
+    sharers = lax.axis_size("walk")
+    width = vectors // count
+    fits = (
+        count == local_walkers and row_block % ROWS == 0 and local_walkers % HALF == 0
+        and width % LANES == 0 and LANES % VECTORS == 0 and width == LANES
+        and electrons <= LANES and orbitals % LANES == 0
+    )
+    if not fits:
+        return plain_body(
+            walkers, correlation_inverse, half_vectors, field_vectors, samples, source
+        )
+    lines = sharers * 2 * local_walkers
+    groups = row_block // ROWS
+    chunks = vectors // VECTORS
+    vmem, anywhere = pltpu.VMEM, pl.ANY
+    dma = pltpu.SemaphoreType.DMA
+    half_type, full_type = jnp.bfloat16, jnp.float32
+    grid = walkers.reshape(local_walkers, 2, row_block, electrons)
+    theta_real, theta_imag = complex_product(
+        grid[:, 0], grid[:, 1], correlation_inverse[:, 0], correlation_inverse[:, 1], "wmk,wkn->wmn"
+    )
+    theta = jnp.stack([theta_real, theta_imag], 0).astype(half_type)
+    theta = theta.reshape(2 * local_walkers, flat)
+    coefficient = call(
+        functools.partial(bias_kernel, count, sharers), 0,
+        jax.ShapeDtypeStruct((count, lines, width), half_type),
+        [vmem, anywhere, vmem],
+        [
+            vmem((count, width, flat), half_type),
+            vmem((sharers, 2 * local_walkers, flat), half_type),
+            vmem((count, lines, width), full_type),
+            vmem((count, lines, width), full_type),
+            dma((count,)), dma((sharers,)), dma((sharers,)),
+            dma((count,)), dma((count,)), dma((count,)), dma((count,)),
+        ],
+    )(theta, half_vectors, samples)
+    columns = jnp.pad(grid.astype(half_type), ((0, 0), (0, 0), (0, 0), (0, LANES - electrons)))
+    columns = columns.transpose(0, 2, 1, 3).reshape(local_walkers, row_block, 2 * LANES)
+    field, whole = call(
+        functools.partial(field_kernel, count, sharers), 1,
+        [
+            jax.ShapeDtypeStruct((2, orbitals, orbitals), half_type),
+            jax.ShapeDtypeStruct((orbitals, 2 * LANES), half_type),
+        ],
+        [vmem, vmem, anywhere],
+        [
+            vmem((chunks, lines * HALF, VECTORS * HALF), half_type),
+            vmem((DEPTH, VECTORS, ROWS, orbitals), half_type),
+            vmem((lines * HALF, 2 * orbitals), full_type),
+            vmem((groups, sharers, local_walkers, 2, ROWS, orbitals), full_type),
+            vmem((groups, sharers, local_walkers, 2, ROWS, orbitals), half_type),
+            vmem((groups, sharers, local_walkers, 2, ROWS, orbitals), half_type),
+            vmem((groups, local_walkers, 2, ROWS, orbitals), half_type),
+            dma((DEPTH,)), dma((count,)), dma((count,)),
+            dma((groups, sharers)), dma((groups, sharers)),
+            dma((groups, count)), dma((groups, count)),
+        ],
+    )(coefficient, columns, field_vectors)
+    moved = call(
+        functools.partial(walker_kernel, count, sharers, electrons), 2,
+        jax.ShapeDtypeStruct((sharers * local_walkers, row_block, 2 * LANES), half_type),
+        [vmem, vmem],
+        [
+            dma((sharers, count)), dma((sharers, count)),
+            vmem((count, row_block, 2 * LANES), half_type),
+        ],
+    )(field, whole)
+    chosen = jnp.take(moved, source, axis=0).reshape(local_walkers, row_block, 2, LANES)
+    chosen = chosen[..., :electrons].transpose(0, 2, 1, 3)
+    return chosen.reshape(local_walkers, 2, flat).astype(walkers.dtype)
+
+
 def solution(mesh):
     placed = (
         P(("groups", "walk"), None, ("chol", "orb")),

time: 241 us -> 86 us (0.36)
  waiting for transfers between devices: 124 us -> 0 us
  Pallas kernels: 0 us -> 74.9 us
  matrix products: 56.9 us -> 5.87 us
  blocking collectives: 21.9 us -> 0 us
  between operations: 13.5 us -> 0.16 us
  starting transfers between devices: 11.1 us -> 0 us
  local copies, waits for them, and re-layouts: 8.36 us -> 3.99 us
  other arithmetic: 3.9 us -> 0.34 us
    pallas_call x0 -> x3, Pallas kernels: none -> 74.9 us  [the longest x1 36.7 us: body(): call(functools.partial(field_kernel, count, sharers), 1, [jax.ShapeDtypeS...]
    psum x1 -> x0, waiting for transfers between devices: 54.5 us -> none  [body(): bias = lax.psum(bias_part, ('chol', 'orb'))]
    dot_general x18 -> x0, matrix products: 40.5 us -> none  [the longest x1 29.4 us: body(): jnp.einsum('wcg,gab->wcab', coefficient, field_vectors, preferred_element...]
    reduce_scatter x1 -> x0, waiting for transfers between devices: 29.1 us -> none  [body(): lax.psum_scatter(field_part, 'walk', scatter_dimension=0, tiled=True)]
    all_gather x1 -> x0, waiting for transfers between devices: 24.6 us -> none  [body(): lax.all_gather(summed.astype(jnp.bfloat16), ('chol', 'orb'), axis=2, tile...]
    all_to_all x2 -> x0, waiting for transfers between devices: 15.7 us -> none  [the longest x1 15.7 us: body(): lax.all_to_all(spread, ('chol', 'orb'), split_axis=0, concat_axis=2, tile...]
    all_gather x2 -> x0, blocking collectives: 12.2 us -> none  [the longest x1 6.27 us: body(): all_theta = lax.all_gather(theta, 'walk', axis=0, tiled=True)]
    all_to_all x2 -> x0, starting transfers between devices: 10.9 us -> none  [the longest x1 5.61 us: body(): lax.all_to_all(parted.astype(jnp.bfloat16), ('chol', 'orb'), split_axis=0...]
  transfers between devices with their start and end apart: 5 -> 0, of which waited for: 4 -> 0; matrix products, arithmetic and copies ran while one was open for 1% -> 0% of each run, Pallas kernels for 0% -> 0%
where the time goes in v1:
time: 86 us; the launch traced here: 85.2 us
  Pallas kernels  74.9 us (87%)
  matrix products  5.87 us (7%)
  local copies, waits for them, and re-layouts  3.99 us (5%)
    pallas_call x1, Pallas kernels, body(): call(functools.partial(field_kernel, count, sharers), 1, [jax.ShapeDtypeS...  36.7 us
    pallas_call x1, Pallas kernels, body(): call(functools.partial(bias_kernel, count, sharers), 0, jax.ShapeDtypeStr...  20.9 us
    pallas_call x1, Pallas kernels, body(): call(functools.partial(walker_kernel, count, sharers, electrons), 2, jax....  17.4 us
    unnamed x5, local copies, waits for them, and re-layouts  1.87 us

profile of v1, /device:TPU:1, one launch (start us, length us, event | category | flops | bytes accessed | tf_op | source)
XLA Modules:
  0.0 85.2 jit_solution(2272605092219863270)
XLA Ops:
  0.0 0.0 copy-start.1
  0.0 1.0 %copy.7 = f32[8,2,4608]{2,0,1:T(8,128)S(1)} copy(f32[8,2,4608]{2,1,0:T(2,128)} %param.6) | data formatting | bytes 589824 | tf_op args[0]
  1.0 0.1 reshape.19
  1.2 1.5 %fusion.8 = f32[8,48,96]{2,1,0:T(8,128)S(1)} fusion(f32[8,2,96,96]{3,2,1,0:T(8,128)} %param.7, f32[8,2,48,96]{3,2,0,1:T(8,128)S(1)} %reshape.19), kind=kOutput, calls=%fused_computation.11 | convolution fusion | flops 42467328 | bytes 737280 | tf_op jit(solution)/shard_map/wmk,wkn->wmn/dot_general | solution.py:19
  2.7 1.5 %fusion.3 = bf16[1,8,48,96]{3,2,1,0:T(8,128)(2,1)S(1)} fusion(f32[8,48,96]{2,1,0:T(8,128)S(1)} %fusion.8, f32[8,2,96,96]{3,2,1,0:T(8,128)} %param.7, f32[8,2,48,96]{3,2,0,1:T(8,128)S(1)} %reshape.19), kind=kOutput, calls=%fused_computation.6 | convolution fusion | flops 42541056 | bytes 860160 | tf_op jit(solution)/shard_map/wmk,wkn->wmn/dot_general | solution.py:20
  4.1 1.5 %fusion.4 = f32[8,48,96]{2,1,0:T(8,128)S(1)} fusion(f32[8,2,96,96]{3,2,1,0:T(8,128)} %param.7, f32[8,2,48,96]{3,2,0,1:T(8,128)S(1)} %reshape.19), kind=kOutput, calls=%fused_computation.7 | convolution fusion | flops 42467328 | bytes 737280 | tf_op jit(solution)/shard_map/wmk,wkn->wmn/dot_general | solution.py:21
  5.6 1.5 %fusion.2 = bf16[1,8,48,96]{3,2,1,0:T(8,128)(2,1)S(1)} fusion(f32[8,48,96]{2,1,0:T(8,128)S(1)} %fusion.4, f32[8,2,96,96]{3,2,1,0:T(8,128)} %param.7, f32[8,2,48,96]{3,2,0,1:T(8,128)S(1)} %reshape.19), kind=kOutput, calls=%fused_computation.5 | convolution fusion | flops 42541056 | bytes 860160 | tf_op jit(solution)/shard_map/wmk,wkn->wmn/dot_general | solution.py:22
  7.1 0.2 convert_element_type.19.theta_ref
  7.3 0.0 copy-start
  7.4 0.8 copy-done
  8.2 20.9 %shard_map.64.coef_ref = bf16[8,32,128]{2,1,0:T(8,128)(2,1)S(1)} custom-call(bf16[16,4608]{1,0:T(8,128)(2,1)S(1)} %convert_element_type.19.theta_ref, bf16[1024,4608]{1,0:T(8,128)(2,1)} %half_ref.1, f32[16,1024]{1,0:T(8,128)S(1)} %copy-done), custom_call_target="tpu_custom_call" | custom-call | tf_op jit(solution)/shard_map/pallas_call | solution.py:502
  29.1 36.7 %shard_map.65 = (bf16[2,384,384]{2,1,0:T(8,128)(2,1)S(1)}, bf16[384,256]{1,0:T(8,128)(2,1)S(1)}) custom-call(bf16[8,32,128]{2,1,0:T(8,128)(2,1)S(1)} %shard_map.64.coef_ref, bf16[8,48,256]{2,1,0:T(8,128)(2,1)S(1)} %copy_bitcast_fusion.columns_ref, bf16[1024,48,384]{2,1,0:T(8,128)(2,1)} %vectors_ref.1), custom_call_target="tpu_custom_call" | custom-call | tf_op jit(solution)/shard_map/pallas_call | solution.py:517
  65.8 17.4 %shard_map.66 = bf16[16,48,256]{2,1,0:T(8,128)(2,1)S(1)} custom-call(bf16[2,384,384]{2,1,0:T(8,128)(2,1)S(1)} %get-tuple-element.7.field_ref, bf16[384,256]{1,0:T(8,128)(2,1)S(1)} %get-tuple-element.8.whole_ref), custom_call_target="tpu_custom_call" | custom-call | tf_op jit(solution)/shard_map/pallas_call | solution.py:537
  83.2 0.0 copy-done.1
  83.2 0.6 gather_fusion
  83.8 0.1 gather.7
  83.9 0.2 convert_bitcast_fusion
  84.1 1.1 %reshape.21 = f32[8,2,4608]{2,1,0:T(2,128)} reshape(f32[8,2,48,96]{3,2,1,0:T(8,128)S(1)} %copy.11) | data formatting | bytes 589824 | tf_op jit(solution)/shard_map/convert_element_type | solution.py:548
  (7 shorter events, 0.2 us)
Async XLA Ops:
  0.0 83.2 %copy-start.1 = (s32[8]{0:T(128)S(1)}, s32[8]{0:T(128)}, u32[]{:S(2)}) copy-start(s32[8]{0:T(128)} %param.11) | copy-start | bytes 100
  7.3 0.8 copy-start

commit v2 on v1

--- a/solution.py
+++ b/solution.py
@@ -136,8 +136,8 @@
 HALF = 8
 ROWS = 16
 VECTORS = 64
-DEPTH = 4
-VMEM_LIMIT = 48 * 1024 * 1024
+DEPTH = 32
+VMEM_LIMIT = 60 * 1024 * 1024
 
 
 def owner_id(index):
@@ -156,10 +156,16 @@
     pl.semaphore_wait(barrier, len(devices))
 
 
-def cross(count, sharers):
+def partners(count, sharers):
     me, walk = position(), lax.axis_index("walk")
-    rows = [owner_id(lax.rem(me + step, count)) for step in range(1, count)]
-    return rows + [{"walk": lax.rem(walk + step, sharers)} for step in range(1, sharers)]
+    others = []
+    for across in range(sharers):
+        for step in range(count):
+            if across + step > 0:
+                target = owner_id(lax.rem(me + step, count))
+                target["walk"] = lax.rem(walk + across, sharers)
+                others.append((across, step, target))
+    return others
 
 
 def remote(source, target, send, recv, device):
@@ -169,7 +175,41 @@
     )
 
 
-def bias_kernel(count, sharers, theta_ref, half_ref, samples_ref, coef_ref,
+def half_load(half_ref, half, load_sem, index):
+    width = half.shape[1]
+    return pltpu.make_async_copy(
+        half_ref.at[pl.ds(pl.multiple_of(index * width, width), width), :],
+        half.at[index], load_sem.at[index],
+    )
+
+
+def block_load(vectors_ref, blocks, load_sem, step):
+    chunks = vectors_ref.shape[0] // VECTORS
+    group, chunk = step // chunks, lax.rem(step, chunks)
+    slot = lax.rem(step, DEPTH)
+    return pltpu.make_async_copy(
+        vectors_ref.at[pl.ds(pl.multiple_of(chunk * VECTORS, VECTORS), VECTORS),
+                       pl.ds(pl.multiple_of(group * ROWS, ROWS), ROWS), :],
+        blocks.at[slot], load_sem.at[slot],
+    )
+
+
+def column_phase(count, columns_ref, whole_ref, column_send, column_recv):
+    me = position()
+    row_block = columns_ref.shape[1]
+    here = pl.ds(pl.multiple_of(me * row_block, ROWS), row_block)
+
+    def send_columns(step, carry):
+        index = lax.rem(me + 1 + step, count)
+        remote(columns_ref.at[index], whole_ref.at[here, :], column_send.at[index],
+               column_recv.at[me], owner_id(index)).start()
+        return carry
+
+    lax.fori_loop(0, count - 1, send_columns, 0)
+    whole_ref[here, :] = columns_ref[me]
+
+
+def bias_phase(count, sharers, theta_ref, half_ref, samples_ref, coef_ref,
                 half, theta, parts, arrived, load_sem, theta_send, theta_recv,
                 part_send, part_recv, coef_send, coef_recv):
     me, walk = position(), lax.axis_index("walk")
@@ -177,17 +217,8 @@
     local = theta_ref.shape[0] // 2
 
     def load(index):
-        return pltpu.make_async_copy(
-            half_ref.at[pl.ds(pl.multiple_of(index * width, width), width), :],
-            half.at[index], load_sem.at[index],
-        )
-
-    def first(step, carry):
-        load(lax.rem(me + 1 + step, count)).start()
-        return carry
-
-    lax.fori_loop(0, count, first, 0)
-    greet(cross(count, sharers))
+        return half_load(half_ref, half, load_sem, index)
+
     sends = []
     for step in range(1, sharers):
         other = lax.rem(walk + step, sharers)
@@ -253,7 +284,7 @@
         send.wait_send()
 
 
-def field_kernel(count, sharers, coef_ref, columns_ref, vectors_ref, field_ref, whole_ref,
+def field_phase(count, sharers, coef_ref, columns_ref, vectors_ref, field_ref, whole_ref,
                  spread, blocks, total, full, outgoing, incoming, finished,
                  load_sem, column_send, column_recv, walk_send, walk_recv,
                  row_send, row_recv):
@@ -268,29 +299,7 @@
     depth = VECTORS * HALF
 
     def load(step):
-        group, chunk = step // chunks, lax.rem(step, chunks)
-        slot = lax.rem(step, DEPTH)
-        return pltpu.make_async_copy(
-            vectors_ref.at[pl.ds(pl.multiple_of(chunk * VECTORS, VECTORS), VECTORS),
-                           pl.ds(pl.multiple_of(group * ROWS, ROWS), ROWS), :],
-            blocks.at[slot], load_sem.at[slot],
-        )
-
-    for step in range(DEPTH - 1):
-        load(jnp.int32(step)).start()
-    greet(cross(count, sharers))
-    here = pl.ds(pl.multiple_of(me * row_block, ROWS), row_block)
-
-    def column_copy(index):
-        return remote(columns_ref.at[index], whole_ref.at[here, :], column_send.at[index],
-                      column_recv.at[me], owner_id(index))
-
-    def send_columns(step, carry):
-        column_copy(lax.rem(me + 1 + step, count)).start()
-        return carry
-
-    lax.fori_loop(0, count - 1, send_columns, 0)
-    whole_ref[here, :] = columns_ref[me]
+        return block_load(vectors_ref, blocks, load_sem, step)
 
     vector_at = lax.broadcasted_iota(jnp.int32, (LANES, depth), 0)
     place = lax.broadcasted_iota(jnp.int32, (LANES, depth), 1)
@@ -375,10 +384,9 @@
 
     def finish(step, carry):
         index = lax.rem(me + 1 + step, count)
-        column_copy(index).wait_send()
         there = pl.ds(pl.multiple_of(index * row_block, ROWS), row_block)
         remote(columns_ref.at[index], whole_ref.at[there, :], column_send.at[index],
-               column_recv.at[index], owner_id(index)).wait_recv()
+               column_recv.at[index], owner_id(index)).wait()
         for group in range(groups):
             row_copy(group, index, False).wait_send()
             row_copy(group, index, True).wait_recv()
@@ -390,24 +398,27 @@
             walk_copy(group, step, False).wait_send()
 
 
-def exact(left, right, dims=(((1,), (0,)), ((), ()))):
-    return lax.dot_general(left, right, dims, precision=lax.Precision.HIGHEST,
-                           preferred_element_type=jnp.float32)
-
-
-def walker_kernel(count, sharers, electrons, field_ref, whole_ref, out_ref,
-                  send_sem, recv_sem, rows):
+def two_parts(value):
+    high = value.astype(jnp.bfloat16)
+    return high, (value - high.astype(jnp.float32)).astype(jnp.bfloat16)
+
+
+def exact(left, right, axis=1):
+    left_high, left_low = two_parts(left)
+    right_high, right_low = two_parts(right)
+    return lax.dot_general(
+        jnp.concatenate([left_high, left_low, left_high], axis=axis),
+        jnp.concatenate([right_high, right_high, right_low], axis=0),
+        (((axis,), (0,)), ((), ())), preferred_element_type=jnp.float32,
+    )
+
+
+def walker_phase(count, sharers, electrons, field_ref, whole_ref, out_ref,
+                 send_sem, recv_sem, rows):
     me, walk = position(), lax.axis_index("walk")
     row_block = rows.shape[1]
     orbitals = field_ref.shape[1]
-    others = []
-    for across in range(sharers):
-        for step in range(count):
-            if across + step > 0:
-                target = owner_id(lax.rem(me + step, count))
-                target["walk"] = lax.rem(walk + across, sharers)
-                others.append((across, step, target))
-    greet([target for _, _, target in others])
+    others = partners(count, sharers)
 
     def swap(value, sign):
         return jnp.concatenate([-sign * value[:, LANES:], sign * value[:, :LANES]], axis=1)
@@ -420,7 +431,7 @@
         imag = jnp.dot(field_ref[1], rounded, preferred_element_type=jnp.float32)
         current = (real + swap(imag, 1.0)) / order_index
         summed = summed + current
-    squares = exact(summed, summed, (((0,), (0,)), ((), ()))) / orbitals
+    squares = exact(summed, summed, 0) / orbitals
     gram_real = squares[:LANES, :LANES] + squares[LANES:, LANES:]
     gram_imag = squares[:LANES, LANES:] - squares[LANES:, :LANES]
     size = 2 * LANES
@@ -455,19 +466,34 @@
                recv_sem.at[across, step], target).wait()
 
 
-def call(kernel, ident, shapes, places, scratch):
-    single = isinstance(shapes, jax.ShapeDtypeStruct)
-    spec = pl.BlockSpec(memory_space=pltpu.VMEM)
-    return pl.pallas_call(
-        kernel,
-        out_shape=shapes,
-        in_specs=[pl.BlockSpec(memory_space=place) for place in places],
-        out_specs=spec if single else [spec] * len(shapes),
-        scratch_shapes=scratch,
-        compiler_params=pltpu.CompilerParams(
-            collective_id=ident, has_side_effects=True, vmem_limit_bytes=VMEM_LIMIT
-        ),
-    )
+def step_kernel(count, sharers, electrons, theta_ref, half_ref, samples_ref, columns_ref,
+                vectors_ref, out_ref, half, theta, parts, arrived, coef, field, whole, spread,
+                blocks, total, full, outgoing, incoming, finished, rows, half_sem, block_sem,
+                theta_send, theta_recv, part_send, part_recv, coef_send, coef_recv,
+                column_send, column_recv, walk_send, walk_recv, row_send, row_recv,
+                out_send, out_recv):
+    me = position()
+
+    def first_half(step, carry):
+        half_load(half_ref, half, half_sem, lax.rem(me + 1 + step, count)).start()
+        return carry
+
+    lax.fori_loop(0, count, first_half, 0)
+
+    def first_blocks(step, carry):
+        block_load(vectors_ref, blocks, block_sem, step).start()
+        return carry
+
+    lax.fori_loop(0, DEPTH - 1, first_blocks, 0)
+    greet([target for _, _, target in partners(count, sharers)])
+    bias_phase(count, sharers, theta_ref, half_ref, samples_ref, coef, half, theta, parts,
+               arrived, half_sem, theta_send, theta_recv, part_send, part_recv, coef_send,
+               coef_recv)
+    column_phase(count, columns_ref, whole, column_send, column_recv)
+    field_phase(count, sharers, coef, columns_ref, vectors_ref, field, whole, spread, blocks,
+                total, full, outgoing, incoming, finished, block_sem, column_send, column_recv,
+                walk_send, walk_recv, row_send, row_recv)
+    walker_phase(count, sharers, electrons, field, whole, out_ref, out_send, out_recv, rows)
 
 
 def body(walkers, correlation_inverse, half_vectors, field_vectors, samples, source):
@@ -482,6 +508,7 @@
         count == local_walkers and row_block % ROWS == 0 and local_walkers % HALF == 0
         and width % LANES == 0 and LANES % VECTORS == 0 and width == LANES
         and electrons <= LANES and orbitals % LANES == 0
+        and (row_block // ROWS) * (vectors // VECTORS) >= DEPTH
     )
     if not fits:
         return plain_body(
@@ -494,34 +521,34 @@
     dma = pltpu.SemaphoreType.DMA
     half_type, full_type = jnp.bfloat16, jnp.float32
     grid = walkers.reshape(local_walkers, 2, row_block, electrons)
-    theta_real, theta_imag = complex_product(
-        grid[:, 0], grid[:, 1], correlation_inverse[:, 0], correlation_inverse[:, 1], "wmk,wkn->wmn"
-    )
-    theta = jnp.stack([theta_real, theta_imag], 0).astype(half_type)
+    pairs = jnp.concatenate([grid[:, 0], grid[:, 1]], axis=2)
+    inverse_real, inverse_imag = correlation_inverse[:, 0], correlation_inverse[:, 1]
+    theta = jnp.stack(
+        [
+            jnp.einsum("wmk,wkn->wmn", pairs, jnp.concatenate(side, axis=1),
+                       precision=lax.Precision.HIGH)
+            for side in ((inverse_real, -inverse_imag), (inverse_imag, inverse_real))
+        ],
+        0,
+    ).astype(half_type)
     theta = theta.reshape(2 * local_walkers, flat)
-    coefficient = call(
-        functools.partial(bias_kernel, count, sharers), 0,
-        jax.ShapeDtypeStruct((count, lines, width), half_type),
-        [vmem, anywhere, vmem],
-        [
+    columns = jnp.pad(grid.astype(half_type), ((0, 0), (0, 0), (0, 0), (0, LANES - electrons)))
+    columns = columns.transpose(0, 2, 1, 3).reshape(local_walkers, row_block, 2 * LANES)
+    moved = pl.pallas_call(
+        functools.partial(step_kernel, count, sharers, electrons),
+        out_shape=jax.ShapeDtypeStruct((sharers * local_walkers, row_block, 2 * LANES), half_type),
+        in_specs=[
+            pl.BlockSpec(memory_space=place) for place in (vmem, anywhere, vmem, vmem, anywhere)
+        ],
+        out_specs=pl.BlockSpec(memory_space=vmem),
+        scratch_shapes=[
             vmem((count, width, flat), half_type),
             vmem((sharers, 2 * local_walkers, flat), half_type),
             vmem((count, lines, width), full_type),
             vmem((count, lines, width), full_type),
-            dma((count,)), dma((sharers,)), dma((sharers,)),
-            dma((count,)), dma((count,)), dma((count,)), dma((count,)),
-        ],
-    )(theta, half_vectors, samples)
-    columns = jnp.pad(grid.astype(half_type), ((0, 0), (0, 0), (0, 0), (0, LANES - electrons)))
-    columns = columns.transpose(0, 2, 1, 3).reshape(local_walkers, row_block, 2 * LANES)
-    field, whole = call(
-        functools.partial(field_kernel, count, sharers), 1,
-        [
-            jax.ShapeDtypeStruct((2, orbitals, orbitals), half_type),
-            jax.ShapeDtypeStruct((orbitals, 2 * LANES), half_type),
-        ],
-        [vmem, vmem, anywhere],
-        [
+            vmem((count, lines, width), half_type),
+            vmem((2, orbitals, orbitals), half_type),
+            vmem((orbitals, 2 * LANES), half_type),
             vmem((chunks, lines * HALF, VECTORS * HALF), half_type),
             vmem((DEPTH, VECTORS, ROWS, orbitals), half_type),
             vmem((lines * HALF, 2 * orbitals), full_type),
@@ -529,20 +556,19 @@
             vmem((groups, sharers, local_walkers, 2, ROWS, orbitals), half_type),
             vmem((groups, sharers, local_walkers, 2, ROWS, orbitals), half_type),
             vmem((groups, local_walkers, 2, ROWS, orbitals), half_type),
-            dma((DEPTH,)), dma((count,)), dma((count,)),
+            vmem((count, row_block, 2 * LANES), half_type),
+            dma((count,)), dma((DEPTH,)),
+            dma((sharers,)), dma((sharers,)),
+            dma((count,)), dma((count,)), dma((count,)), dma((count,)),
+            dma((count,)), dma((count,)),
             dma((groups, sharers)), dma((groups, sharers)),
             dma((groups, count)), dma((groups, count)),
+            dma((sharers, count)), dma((sharers, count)),
         ],
-    )(coefficient, columns, field_vectors)
-    moved = call(
-        functools.partial(walker_kernel, count, sharers, electrons), 2,
-        jax.ShapeDtypeStruct((sharers * local_walkers, row_block, 2 * LANES), half_type),
-        [vmem, vmem],
-        [
-            dma((sharers, count)), dma((sharers, count)),
-            vmem((count, row_block, 2 * LANES), half_type),
-        ],
-    )(field, whole)
+        compiler_params=pltpu.CompilerParams(
+            collective_id=0, has_side_effects=True, vmem_limit_bytes=VMEM_LIMIT
+        ),
+    )(theta, half_vectors, samples, columns, field_vectors)
     chosen = jnp.take(moved, source, axis=0).reshape(local_walkers, row_block, 2, LANES)
     chosen = chosen[..., :electrons].transpose(0, 2, 1, 3)
     return chosen.reshape(local_walkers, 2, flat).astype(walkers.dtype)

time: 86 us -> 80 us (0.930)
  matrix products: 5.87 us -> 1.07 us
  Pallas kernels: 74.9 us -> 70.5 us
  local copies, waits for them, and re-layouts: 3.99 us -> 6.69 us
  other arithmetic: 0.34 us -> 1.37 us
    dot_general x4 -> x2, matrix products: 5.87 us -> 1.07 us  [body(): jnp.einsum('wmk,wkn->wmn', pairs, jnp.concatenate(side, axis=1), precisio...]
    pallas_call x3 -> x1, Pallas kernels: 74.9 us -> 70.5 us  [body(): pl.pallas_call(functools.partial(step_kernel, count, sharers, electrons),...]
    squeeze x0 -> x2, local copies, waits for them, and re-layouts: none -> 1.2 us  [the longest x1 1.18 us: body(): correlation_inverse[:, 1]]
    neg x0 -> x1, other arithmetic: none -> 1.03 us  [body(): -inverse_imag]
    gather x2, local copies, waits for them, and re-layouts: 0.61 us -> 1.61 us  [body(): jnp.take(moved, source, axis=0).reshape(local_walkers, row_block, 2, LANES)]
    unnamed x5 -> x3, local copies, waits for them, and re-layouts: 1.87 us -> 1.04 us
where the time goes in v2:
time: 80 us; the launch traced here: 79.7 us
  Pallas kernels  70.5 us (88%)
  local copies, waits for them, and re-layouts  6.69 us (8%)
  other arithmetic  1.37 us (2%)
  matrix products  1.07 us (1%)
    pallas_call x1, Pallas kernels, body(): pl.pallas_call(functools.partial(step_kernel, count, sharers, electrons),...  70.5 us
    gather x2, local copies, waits for them, and re-layouts, body(): jnp.take(moved, source, axis=0).reshape(local_walkers, row_block, 2, LANES)  1.61 us

profile of v2, /device:TPU:1, one launch (start us, length us, event | category | flops | bytes accessed | tf_op | source)
XLA Modules:
  0.0 79.7 jit_solution(18337145602232214994)
XLA Ops:
  0.0 0.0 copy-start
  0.0 1.0 %copy.7 = f32[8,2,4608]{2,0,1:T(8,128)S(1)} copy(f32[8,2,4608]{2,1,0:T(2,128)} %param.6) | data formatting | bytes 589824 | tf_op args[0]
  1.0 0.1 reshape.19
  1.2 1.2 %slice_bitcast_fusion = (f32[8,96,96]{2,1,0:T(8,128)S(1)}, f32[8,96,96]{2,1,0:T(8,128)S(1)}) fusion(f32[8,2,96,96]{3,2,1,0:T(8,128)} %param.7), kind=kLoop, calls=%fused_computation.13 | loop fusion | bytes 1179648 | tf_op jit(solution)/shard_map/squeeze | solution.py:525
  2.4 0.5 fusion.1
  3.0 1.0 %fusion.10 = f32[8,96,96]{2,1,0:T(8,128)S(1)} fusion(f32[8,2,96,96]{3,2,1,0:T(8,128)} %param.7), kind=kLoop, calls=%fused_computation.26 | loop fusion | flops 73728 | bytes 589824 | tf_op jit(solution)/shard_map/neg | solution.py:530
  4.0 0.5 fusion
  4.6 0.9 %convert_element_type.19.theta_ref = bf16[16,4608]{1,0:T(8,128)(2,1)} reshape(bf16[2,8,48,96]{3,2,1,0:T(8,128)(2,1)S(1)} %pad_maximum_fusion.3) | data formatting | bytes 294912 | tf_op jit(solution)/shard_map/convert_element_type | solution.py:533
  5.5 0.7 copy_bitcast_fusion.columns_ref
  6.2 70.5 %shard_map.64 = bf16[16,48,256]{2,1,0:T(8,128)(2,1)} custom-call(bf16[16,4608]{1,0:T(8,128)(2,1)} %convert_element_type.19.theta_ref, bf16[1024,4608]{1,0:T(8,128)(2,1)} %half_ref.1, f32[16,1024]{1,0:T(8,128)} %samples_ref.1, bf16[8,48,256]{2,1,0:T(8,128)(2,1)} %copy_bitcast_fusion.columns_ref, bf16[1024,48,384]{2,1,0:T(8,128)(2,1)} %vectors_ref.1), custom_call_target="tpu_custom_call" | custom-call | tf_op jit(solution)/shard_map/pallas_call | solution.py:537
  76.7 0.0 copy-done
  76.7 1.6 %gather_fusion = bf16[8,48,256]{2,1,0:T(8,128)(2,1)S(1)} fusion(bf16[16,48,256]{2,1,0:T(8,128)(2,1)} %shard_map.64, s32[1024]{0:T(1024)S(1)} %pad_clamp_fusion), kind=kCustom, calls=%fused_computation | custom fusion | bytes 393248 | tf_op jit(solution)/shard_map/jit(_take)/gather | solution.py:572
  78.3 0.1 gather.7
  78.3 0.2 convert_bitcast_fusion
  78.6 1.1 %reshape.21 = f32[8,2,4608]{2,1,0:T(2,128)} reshape(f32[8,2,48,96]{3,2,1,0:T(8,128)S(1)} %copy.11) | data formatting | bytes 589824 | tf_op jit(solution)/shard_map/convert_element_type | solution.py:574
  (7 shorter events, 0.1 us)
Async XLA Ops:
  0.0 76.7 %copy-start = (s32[8]{0:T(128)S(1)}, s32[8]{0:T(128)}, u32[]{:S(2)}) copy-start(s32[8]{0:T(128)} %param.11) | copy-start | bytes 100

commit v3 on v2

--- a/solution.py
+++ b/solution.py
@@ -135,8 +135,9 @@
 LANES = 128
 HALF = 8
 ROWS = 16
-VECTORS = 64
-DEPTH = 32
+VECTORS = 128
+DEPTH = 48
+LAG = 2
 VMEM_LIMIT = 60 * 1024 * 1024
 
 
@@ -153,7 +154,7 @@
     barrier = pltpu.get_barrier_semaphore()
     for device in devices:
         pl.semaphore_signal(barrier, inc=1, device_id=device, device_id_type=MESH)
-    pl.semaphore_wait(barrier, len(devices))
+    return barrier
 
 
 def partners(count, sharers):
@@ -175,6 +176,37 @@
     )
 
 
+def piece_at(across, piece, base):
+    rows = pl.ds(pl.multiple_of(base + (piece // across) * ROWS, ROWS), ROWS)
+    return rows, pl.ds(pl.multiple_of(lax.rem(piece, across) * LANES, LANES), LANES)
+
+
+def theta_phase(columns_ref, inverse_ref, theta, columns, matrix, grid):
+    walk = lax.axis_index("walk")
+    local, row_block = columns_ref.shape[0], columns_ref.shape[1]
+    electrons = inverse_ref.shape[2]
+    matrix[...] = jnp.zeros_like(matrix)
+    for walker in range(local):
+        real, imag = inverse_ref[walker, 0], inverse_ref[walker, 1]
+        matrix[:electrons, :electrons] = real
+        matrix[:electrons, LANES:LANES + electrons] = imag
+        matrix[LANES:LANES + electrons, :electrons] = -imag
+        matrix[LANES:LANES + electrons, LANES:LANES + electrons] = real
+        rotated = exact(columns_ref[walker], matrix[...])
+        grid[:, walker, :] = rotated[:, :LANES]
+        grid[:, local + walker, :] = rotated[:, LANES:]
+        columns[walker] = columns_ref[walker].astype(jnp.bfloat16)
+    lane = lax.broadcasted_iota(jnp.int32, (2 * local, LANES), 1)
+    for tile in range(row_block * electrons // LANES):
+        start = tile * LANES
+        value = None
+        for row in range(start // electrons, (start + LANES - 1) // electrons + 1):
+            moved = pltpu.roll(grid[row], row * electrons % LANES, 1)
+            value = moved if value is None else jnp.where(
+                lane < row * electrons - start, value, moved)
+        theta[walk, :, start:start + LANES] = value.astype(jnp.bfloat16)
+
+
 def half_load(half_ref, half, load_sem, index):
     width = half.shape[1]
     return pltpu.make_async_copy(
@@ -185,11 +217,10 @@
 
 def block_load(vectors_ref, blocks, load_sem, step):
     chunks = vectors_ref.shape[0] // VECTORS
-    group, chunk = step // chunks, lax.rem(step, chunks)
-    slot = lax.rem(step, DEPTH)
+    rows, lanes = piece_at(vectors_ref.shape[2] // LANES, step // chunks, 0)
+    chunk, slot = lax.rem(step, chunks), lax.rem(step, DEPTH)
     return pltpu.make_async_copy(
-        vectors_ref.at[pl.ds(pl.multiple_of(chunk * VECTORS, VECTORS), VECTORS),
-                       pl.ds(pl.multiple_of(group * ROWS, ROWS), ROWS), :],
+        vectors_ref.at[pl.ds(pl.multiple_of(chunk * VECTORS, VECTORS), VECTORS), rows, lanes],
         blocks.at[slot], load_sem.at[slot],
     )
 
@@ -209,12 +240,12 @@
     whole_ref[here, :] = columns_ref[me]
 
 
-def bias_phase(count, sharers, theta_ref, half_ref, samples_ref, coef_ref,
+def bias_phase(count, sharers, half_ref, samples_ref, coef_ref,
                 half, theta, parts, arrived, load_sem, theta_send, theta_recv,
                 part_send, part_recv, coef_send, coef_recv):
     me, walk = position(), lax.axis_index("walk")
     width = half.shape[1]
-    local = theta_ref.shape[0] // 2
+    local = theta.shape[1] // 2
 
     def load(index):
         return half_load(half_ref, half, load_sem, index)
@@ -222,13 +253,12 @@
     sends = []
     for step in range(1, sharers):
         other = lax.rem(walk + step, sharers)
-        sends.append(remote(theta_ref, theta.at[walk], theta_send.at[step],
+        sends.append(remote(theta.at[walk], theta.at[walk], theta_send.at[step],
                             theta_recv.at[walk], {"walk": other}))
         sends[-1].start()
-    theta[walk] = theta_ref[...]
     for step in range(1, sharers):
         other = lax.rem(walk + step, sharers)
-        remote(theta_ref, theta.at[other], theta_send.at[step],
+        remote(theta.at[walk], theta.at[other], theta_send.at[step],
                theta_recv.at[other], {"walk": other}).wait_recv()
 
     def product(index):
@@ -293,10 +323,11 @@
     row_block = columns_ref.shape[1]
     orbitals = vectors_ref.shape[2]
     chunks = vectors_ref.shape[0] // VECTORS
-    groups = row_block // ROWS
     lines = coef_ref.shape[1]
     per_block = coef_ref.shape[2] // VECTORS
     depth = VECTORS * HALF
+    across = orbitals // LANES
+    pieces = (row_block // ROWS) * across
 
     def load(step):
         return block_load(vectors_ref, blocks, load_sem, step)
@@ -320,82 +351,95 @@
 
         lax.fori_loop(0, coef_ref.shape[0], widen, 0)
 
-    def walk_copy(group, step, arriving):
-        other = lax.rem(walk + step, sharers) if not arriving else lax.rem(
-            walk + sharers - step, sharers)
-        return remote(outgoing.at[group, other], incoming.at[group, other if arriving else walk],
-                      walk_send.at[group, other], walk_recv.at[group, other if arriving else walk],
-                      {"walk": other})
-
-    def row_copy(group, index, arriving):
+    def walk_copy(piece, step, arriving):
+        other = lax.rem(walk + (sharers - step if arriving else step), sharers)
+        giver = other if arriving else walk
+        return remote(outgoing.at[piece, other], incoming.at[piece, giver],
+                      walk_send.at[piece, other], walk_recv.at[piece, giver], {"walk": other})
+
+    def row_copy(piece, index, arriving):
         giver = index if arriving else me
-        at = pl.ds(pl.multiple_of(giver * row_block + group * ROWS, ROWS), ROWS)
-        return remote(finished.at[group, index], field_ref.at[:, at, :],
-                      row_send.at[group, index], row_recv.at[group, giver], owner_id(index))
-
-    def deliver(group):
-        result = full[group, walk]
+        rows, lanes = piece_at(across, piece, giver * row_block)
+        return remote(finished.at[piece, index], field_ref.at[:, rows, lanes],
+                      row_send.at[piece, index], row_recv.at[piece, giver], owner_id(index))
+
+    def deliver(piece):
+        result = full[piece, walk]
         for step in range(1, sharers):
-            walk_copy(group, step, True).wait_recv()
+            walk_copy(piece, step, True).wait_recv()
             other = lax.rem(walk + sharers - step, sharers)
-            result = result + incoming[group, other].astype(jnp.float32)
-        finished[group] = result.astype(jnp.bfloat16)
+            result = result + incoming[piece, other].astype(jnp.float32)
+        finished[piece] = result.astype(jnp.bfloat16)
 
         def send_rows(step, carry):
-            row_copy(group, lax.rem(me + 1 + step, count), False).start()
+            row_copy(piece, lax.rem(me + 1 + step, count), False).start()
             return carry
 
         lax.fori_loop(0, count - 1, send_rows, 0)
-        field_ref[:, pl.ds(pl.multiple_of(me * row_block + group * ROWS, ROWS), ROWS), :] = (
-            finished[group, me]
-        )
-
-    for group in range(groups):
+        rows, lanes = piece_at(across, piece, me * row_block)
+        field_ref[:, rows, lanes] = finished[piece, me]
+
+    def one_piece(piece, carry):
         total[...] = jnp.zeros_like(total)
 
-        def add(chunk, carry):
-            step = group * chunks + chunk
-
-            @pl.when(step + DEPTH - 1 < groups * chunks)
+        def add(chunk, inner):
+            step = piece * chunks + chunk
+
+            @pl.when(step + DEPTH - 1 < pieces * chunks)
             def _():
                 load(step + DEPTH - 1).start()
 
             load(step).wait()
             block = blocks[lax.rem(step, DEPTH)]
-            upper = block[:, :HALF, :].reshape(depth, orbitals)
-            lower = block[:, HALF:, :].reshape(depth, orbitals)
+            upper = block[:, :HALF, :].reshape(depth, LANES)
+            lower = block[:, HALF:, :].reshape(depth, LANES)
             total[...] += jnp.dot(
                 spread[chunk], jnp.concatenate([upper, lower], axis=1),
                 preferred_element_type=jnp.float32,
             )
-            return carry
+            return inner
 
         lax.fori_loop(0, chunks, add, 0)
-        result = total[...].reshape(sharers, 2, local, HALF, 2 * orbitals)
-        result = jnp.concatenate([result[..., :orbitals], result[..., orbitals:]], axis=3)
+        result = total[...].reshape(sharers, 2, local, HALF, 2 * LANES)
+        result = jnp.concatenate([result[..., :LANES], result[..., LANES:]], axis=3)
         for part in range(2):
-            full[group, :, :, part] = result[:, part]
-            outgoing[group, :, :, part] = result[:, part].astype(jnp.bfloat16)
+            full[piece, :, :, part] = result[:, part]
+            outgoing[piece, :, :, part] = result[:, part].astype(jnp.bfloat16)
         for step in range(1, sharers):
-            walk_copy(group, step, False).start()
-        if group > 0:
-            deliver(group - 1)
-    deliver(groups - 1)
+            walk_copy(piece, step, False).start()
+
+        @pl.when(piece >= LAG)
+        def _():
+            deliver(piece - LAG)
+
+        return carry
+
+    lax.fori_loop(0, pieces, one_piece, 0)
+    for piece in range(pieces - LAG, pieces):
+        deliver(piece)
 
     def finish(step, carry):
         index = lax.rem(me + 1 + step, count)
         there = pl.ds(pl.multiple_of(index * row_block, ROWS), row_block)
         remote(columns_ref.at[index], whole_ref.at[there, :], column_send.at[index],
                column_recv.at[index], owner_id(index)).wait()
-        for group in range(groups):
-            row_copy(group, index, False).wait_send()
-            row_copy(group, index, True).wait_recv()
+
+        def pieces_of(piece, inner):
+            row_copy(piece, index, False).wait_send()
+            row_copy(piece, index, True).wait_recv()
+            return inner
+
+        lax.fori_loop(0, pieces, pieces_of, 0)
         return carry
 
     lax.fori_loop(0, count - 1, finish, 0)
-    for group in range(groups):
+
+    def close(piece, carry):
         for step in range(1, sharers):
-            walk_copy(group, step, False).wait_send()
+            walk_copy(piece, step, False).wait_send()
+        return carry
+
+    lax.fori_loop(0, pieces, close, 0)
 
 
 def two_parts(value):
@@ -466,8 +510,8 @@
                recv_sem.at[across, step], target).wait()
 
 
-def step_kernel(count, sharers, electrons, theta_ref, half_ref, samples_ref, columns_ref,
-                vectors_ref, out_ref, half, theta, parts, arrived, coef, field, whole, spread,
+def step_kernel(count, sharers, electrons, columns_ref, inverse_ref, half_ref, samples_ref,
+                vectors_ref, out_ref, columns, matrix, grid, half, theta, parts, arrived, coef, field, whole, spread,
                 blocks, total, full, outgoing, incoming, finished, rows, half_sem, block_sem,
                 theta_send, theta_recv, part_send, part_recv, coef_send, coef_recv,
                 column_send, column_recv, walk_send, walk_recv, row_send, row_recv,
@@ -485,12 +529,15 @@
         return carry
 
     lax.fori_loop(0, DEPTH - 1, first_blocks, 0)
-    greet([target for _, _, target in partners(count, sharers)])
-    bias_phase(count, sharers, theta_ref, half_ref, samples_ref, coef, half, theta, parts,
+    others = [target for _, _, target in partners(count, sharers)]
+    barrier = greet(others)
+    theta_phase(columns_ref, inverse_ref, theta, columns, matrix, grid)
+    pl.semaphore_wait(barrier, len(others))
+    bias_phase(count, sharers, half_ref, samples_ref, coef, half, theta, parts,
                arrived, half_sem, theta_send, theta_recv, part_send, part_recv, coef_send,
                coef_recv)
-    column_phase(count, columns_ref, whole, column_send, column_recv)
-    field_phase(count, sharers, coef, columns_ref, vectors_ref, field, whole, spread, blocks,
+    column_phase(count, columns, whole, column_send, column_recv)
+    field_phase(count, sharers, coef, columns, vectors_ref, field, whole, spread, blocks,
                 total, full, outgoing, incoming, finished, block_sem, column_send, column_recv,
                 walk_send, walk_recv, row_send, row_recv)
     walker_phase(count, sharers, electrons, field, whole, out_ref, out_send, out_recv, rows)
@@ -508,40 +555,33 @@
         count == local_walkers and row_block % ROWS == 0 and local_walkers % HALF == 0
         and width % LANES == 0 and LANES % VECTORS == 0 and width == LANES
         and electrons <= LANES and orbitals % LANES == 0
-        and (row_block // ROWS) * (vectors // VECTORS) >= DEPTH
+        and flat % LANES == 0
+        and (row_block // ROWS) * (orbitals // LANES) * (vectors // VECTORS) >= DEPTH
     )
     if not fits:
         return plain_body(
             walkers, correlation_inverse, half_vectors, field_vectors, samples, source
         )
     lines = sharers * 2 * local_walkers
-    groups = row_block // ROWS
+    pieces = (row_block // ROWS) * (orbitals // LANES)
     chunks = vectors // VECTORS
     vmem, anywhere = pltpu.VMEM, pl.ANY
     dma = pltpu.SemaphoreType.DMA
     half_type, full_type = jnp.bfloat16, jnp.float32
     grid = walkers.reshape(local_walkers, 2, row_block, electrons)
-    pairs = jnp.concatenate([grid[:, 0], grid[:, 1]], axis=2)
-    inverse_real, inverse_imag = correlation_inverse[:, 0], correlation_inverse[:, 1]
-    theta = jnp.stack(
-        [
-            jnp.einsum("wmk,wkn->wmn", pairs, jnp.concatenate(side, axis=1),
-                       precision=lax.Precision.HIGH)
-            for side in ((inverse_real, -inverse_imag), (inverse_imag, inverse_real))
-        ],
-        0,
-    ).astype(half_type)
-    theta = theta.reshape(2 * local_walkers, flat)
-    columns = jnp.pad(grid.astype(half_type), ((0, 0), (0, 0), (0, 0), (0, LANES - electrons)))
+    columns = jnp.pad(grid, ((0, 0), (0, 0), (0, 0), (0, LANES - electrons)))
     columns = columns.transpose(0, 2, 1, 3).reshape(local_walkers, row_block, 2 * LANES)
     moved = pl.pallas_call(
         functools.partial(step_kernel, count, sharers, electrons),
         out_shape=jax.ShapeDtypeStruct((sharers * local_walkers, row_block, 2 * LANES), half_type),
         in_specs=[
-            pl.BlockSpec(memory_space=place) for place in (vmem, anywhere, vmem, vmem, anywhere)
+            pl.BlockSpec(memory_space=place) for place in (vmem, vmem, anywhere, vmem, anywhere)
         ],
         out_specs=pl.BlockSpec(memory_space=vmem),
         scratch_shapes=[
+            vmem((local_walkers, row_block, 2 * LANES), half_type),
+            vmem((2 * LANES, 2 * LANES), full_type),
+            vmem((row_block, 2 * local_walkers, LANES), full_type),
             vmem((count, width, flat), half_type),
             vmem((sharers, 2 * local_walkers, flat), half_type),
             vmem((count, lines, width), full_type),
@@ -550,25 +590,25 @@
             vmem((2, orbitals, orbitals), half_type),
             vmem((orbitals, 2 * LANES), half_type),
             vmem((chunks, lines * HALF, VECTORS * HALF), half_type),
-            vmem((DEPTH, VECTORS, ROWS, orbitals), half_type),
-            vmem((lines * HALF, 2 * orbitals), full_type),
-            vmem((groups, sharers, local_walkers, 2, ROWS, orbitals), full_type),
-            vmem((groups, sharers, local_walkers, 2, ROWS, orbitals), half_type),
-            vmem((groups, sharers, local_walkers, 2, ROWS, orbitals), half_type),
-            vmem((groups, local_walkers, 2, ROWS, orbitals), half_type),
+            vmem((DEPTH, VECTORS, ROWS, LANES), half_type),
+            vmem((lines * HALF, 2 * LANES), full_type),
+            vmem((pieces, sharers, local_walkers, 2, ROWS, LANES), full_type),
+            vmem((pieces, sharers, local_walkers, 2, ROWS, LANES), half_type),
+            vmem((pieces, sharers, local_walkers, 2, ROWS, LANES), half_type),
+            vmem((pieces, local_walkers, 2, ROWS, LANES), half_type),
             vmem((count, row_block, 2 * LANES), half_type),
             dma((count,)), dma((DEPTH,)),
             dma((sharers,)), dma((sharers,)),
             dma((count,)), dma((count,)), dma((count,)), dma((count,)),
             dma((count,)), dma((count,)),
-            dma((groups, sharers)), dma((groups, sharers)),
-            dma((groups, count)), dma((groups, count)),
+            dma((pieces, sharers)), dma((pieces, sharers)),
+            dma((pieces, count)), dma((pieces, count)),
             dma((sharers, count)), dma((sharers, count)),
         ],
         compiler_params=pltpu.CompilerParams(
             collective_id=0, has_side_effects=True, vmem_limit_bytes=VMEM_LIMIT
         ),
-    )(theta, half_vectors, samples, columns, field_vectors)
+    )(columns, correlation_inverse, half_vectors, samples, field_vectors)
     chosen = jnp.take(moved, source, axis=0).reshape(local_walkers, row_block, 2, LANES)
     chosen = chosen[..., :electrons].transpose(0, 2, 1, 3)
     return chosen.reshape(local_walkers, 2, flat).astype(walkers.dtype)

time: 80 us -> 81.3 us (1.016)
  Pallas kernels: 70.5 us -> 75.2 us
  local copies, waits for them, and re-layouts: 6.69 us -> 5.44 us
  other arithmetic: 1.37 us -> 0.26 us
  matrix products: 1.07 us -> 0 us
    pallas_call x1, Pallas kernels: 70.5 us -> 75.2 us  [body(): pl.pallas_call(functools.partial(step_kernel, count, sharers, electrons),...]
    reshape x1 -> x2, local copies, waits for them, and re-layouts: 0.14 us -> 1.46 us  [body(): grid = walkers.reshape(local_walkers, 2, row_block, electrons)]
    squeeze x2 -> x0, local copies, waits for them, and re-layouts: 1.2 us -> none  [the longest x1 1.18 us: body(): correlation_inverse[:, 1]]
    dot_general x2 -> x0, matrix products: 1.07 us -> none  [body(): jnp.einsum('wmk,wkn->wmn', pairs, jnp.concatenate(side, axis=1), precisio...]
    unnamed x3 -> x2, local copies, waits for them, and re-layouts: 1.04 us -> 0.01 us
    neg x1 -> x0, other arithmetic: 1.03 us -> none  [body(): -inverse_imag]
    convert_element_type x1 -> x0, local copies, waits for them, and re-layouts: 0.86 us -> none  [body(): theta = jnp.stack([jnp.einsum('wmk,wkn->wmn', pairs, jnp.concatenate(side...]
where the time goes in v3:
time: 81.3 us; the launch traced here: 81 us
  Pallas kernels  75.2 us (92%)
  local copies, waits for them, and re-layouts  5.44 us (7%)
    pallas_call x1, Pallas kernels, body(): pl.pallas_call(functools.partial(step_kernel, count, sharers, electrons),...  75.2 us

profile of v3, /device:TPU:1, one launch (start us, length us, event | category | flops | bytes accessed | tf_op | source)
XLA Modules:
  0.0 81.0 jit_solution(11726895287906581807)
XLA Ops:
  0.0 0.0 copy-start
  0.0 1.3 %reshape.16 = f32[8,2,48,96]{3,2,1,0:T(8,128)S(1)} reshape(f32[8,2,4608]{2,1,0:T(2,128)} %param.6) | data formatting | bytes 589824 | tf_op jit(solution)/shard_map/reshape | solution.py:571
  1.3 0.2 copy.7
  1.5 0.2 pad_bitcast_fusion
  1.7 1.0 %reshape.17.columns_ref = f32[8,48,256]{2,1,0:T(8,128)} reshape(f32[8,48,2,128]{3,2,1,0:T(2,128)S(1)} %pad_bitcast_fusion) | data formatting | bytes 786432 | tf_op jit(solution)/shard_map/reshape | solution.py:573
  2.7 75.2 %shard_map.64 = bf16[16,48,256]{2,1,0:T(8,128)(2,1)} custom-call(f32[8,48,256]{2,1,0:T(8,128)} %reshape.17.columns_ref, f32[8,2,96,96]{3,2,1,0:T(8,128)} %inverse_ref.1, bf16[1024,4608]{1,0:T(8,128)(2,1)} %half_ref.1, f32[16,1024]{1,0:T(8,128)} %samples_ref.1, bf16[1024,48,384]{2,1,0:T(8,128)(2,1)} %vectors_ref.1), custom_call_target="tpu_custom_call" | custom-call | tf_op jit(solution)/shard_map/pallas_call | solution.py:574
  78.0 0.0 copy-done
  78.0 1.6 %gather_fusion = bf16[8,48,256]{2,1,0:T(8,128)(2,1)S(1)} fusion(bf16[16,48,256]{2,1,0:T(8,128)(2,1)} %shard_map.64, s32[1024]{0:T(1024)S(1)} %pad_clamp_fusion), kind=kCustom, calls=%fused_computation | custom fusion | bytes 393248 | tf_op jit(solution)/shard_map/jit(_take)/gather | solution.py:612
  79.6 0.1 gather.7
  79.7 0.2 convert_bitcast_fusion
  79.9 1.1 %reshape.18 = f32[8,2,4608]{2,1,0:T(2,128)} reshape(f32[8,2,48,96]{3,2,1,0:T(8,128)S(1)} %copy.8) | data formatting | bytes 589824 | tf_op jit(solution)/shard_map/convert_element_type | solution.py:614
  (4 shorter events, 0.0 us)
Async XLA Ops:
  0.0 78.0 %copy-start = (s32[8]{0:T(128)S(1)}, s32[8]{0:T(128)}, u32[]{:S(2)}) copy-start(s32[8]{0:T(128)} %param.11) | copy-start | bytes 100

commit v4 on v2

--- a/solution.py
+++ b/solution.py
@@ -135,8 +135,8 @@
 LANES = 128
 HALF = 8
 ROWS = 16
-VECTORS = 64
-DEPTH = 32
+VECTORS = 128
+DEPTH = 16
 VMEM_LIMIT = 60 * 1024 * 1024
 
 
@@ -153,7 +153,7 @@
     barrier = pltpu.get_barrier_semaphore()
     for device in devices:
         pl.semaphore_signal(barrier, inc=1, device_id=device, device_id_type=MESH)
-    pl.semaphore_wait(barrier, len(devices))
+    return barrier
 
 
 def partners(count, sharers):
@@ -175,6 +175,39 @@
     )
 
 
+def theta_phase(columns_ref, inverse_ref, theta, columns, matrices, grid):
+    walk = lax.axis_index("walk")
+    local, row_block = columns_ref.shape[0], columns_ref.shape[1]
+    electrons = inverse_ref.shape[2]
+    size = 2 * LANES
+    matrices[...] = jnp.zeros_like(matrices)
+    for walker in range(local):
+        matrix = matrices.at[walker % 2]
+        real_parts = two_parts(inverse_ref[walker, 0])
+        imag_parts = two_parts(inverse_ref[walker, 1])
+        for place, part in enumerate((0, 0, 1)):
+            first, second = place * size, place * size + LANES
+            matrix[first:first + electrons, :electrons] = real_parts[part]
+            matrix[first:first + electrons, LANES:LANES + electrons] = imag_parts[part]
+            matrix[second:second + electrons, :electrons] = -imag_parts[part]
+            matrix[second:second + electrons, LANES:LANES + electrons] = real_parts[part]
+        high, low = two_parts(columns_ref[walker])
+        columns[walker] = high
+        rotated = jnp.dot(jnp.concatenate([high, low, high], axis=1), matrix[...],
+                          preferred_element_type=jnp.float32)
+        grid[:, walker, :] = rotated[:, :LANES]
+        grid[:, local + walker, :] = rotated[:, LANES:]
+    lane = lax.broadcasted_iota(jnp.int32, (2 * local, LANES), 1)
+    for tile in range(row_block * electrons // LANES):
+        start = tile * LANES
+        value = None
+        for row in range(start // electrons, (start + LANES - 1) // electrons + 1):
+            moved = pltpu.roll(grid[row], row * electrons % LANES, 1)
+            value = moved if value is None else jnp.where(
+                lane < row * electrons - start, value, moved)
+        theta[walk, :, start:start + LANES] = value.astype(jnp.bfloat16)
+
+
 def half_load(half_ref, half, load_sem, index):
     width = half.shape[1]
     return pltpu.make_async_copy(
@@ -209,12 +242,12 @@
     whole_ref[here, :] = columns_ref[me]
 
 
-def bias_phase(count, sharers, theta_ref, half_ref, samples_ref, coef_ref,
+def bias_phase(count, sharers, half_ref, samples_ref, coef_ref,
                 half, theta, parts, arrived, load_sem, theta_send, theta_recv,
                 part_send, part_recv, coef_send, coef_recv):
     me, walk = position(), lax.axis_index("walk")
     width = half.shape[1]
-    local = theta_ref.shape[0] // 2
+    local = theta.shape[1] // 2
 
     def load(index):
         return half_load(half_ref, half, load_sem, index)
@@ -222,34 +255,43 @@
     sends = []
     for step in range(1, sharers):
         other = lax.rem(walk + step, sharers)
-        sends.append(remote(theta_ref, theta.at[walk], theta_send.at[step],
+        sends.append(remote(theta.at[walk], theta.at[walk], theta_send.at[step],
                             theta_recv.at[walk], {"walk": other}))
         sends[-1].start()
-    theta[walk] = theta_ref[...]
     for step in range(1, sharers):
         other = lax.rem(walk + step, sharers)
-        remote(theta_ref, theta.at[other], theta_send.at[step],
+        remote(theta.at[walk], theta.at[other], theta_send.at[step],
                theta_recv.at[other], {"walk": other}).wait_recv()
-
-    def product(index):
-        load(index).wait()
-        return lax.dot_general(
-            theta[...].reshape(sharers * 2 * local, theta.shape[2]), half[index],
-            (((1,), (1,)), ((), ())), preferred_element_type=jnp.float32,
-        )
 
     def part_copy(index):
         return remote(parts.at[index], arrived.at[me], part_send.at[index],
                       part_recv.at[me], owner_id(index))
 
     def one(step, carry):
-        index = lax.rem(me + 1 + step, count)
-        parts[index] = product(index)
-        part_copy(index).start()
-        return carry
-
-    lax.fori_loop(0, count - 1, one, 0)
-    arrived[me] = product(me)
+        pair = lax.rem(me // 2 + 1 + step, count // 2)
+        for side in range(2):
+            load(pair * 2 + side).wait()
+        product = lax.dot_general(
+            theta[...].reshape(sharers * 2 * local, theta.shape[2]),
+            half[pl.ds(pair * 2, 2)].reshape(2 * width, theta.shape[2]),
+            (((1,), (1,)), ((), ())), preferred_element_type=jnp.float32,
+        )
+        for side in range(2):
+            index = pair * 2 + side
+            value = product[:, side * width:(side + 1) * width]
+
+            @pl.when(index == me)
+            def _():
+                arrived[me] = value
+
+            @pl.when(index != me)
+            def _():
+                parts[index] = value
+                part_copy(index).start()
+
+        return carry
+
+    lax.fori_loop(0, count // 2, one, 0)
 
     def take(step, carry):
         index = lax.rem(me + 1 + step, count)
@@ -361,9 +403,9 @@
                 load(step + DEPTH - 1).start()
 
             load(step).wait()
-            block = blocks[lax.rem(step, DEPTH)]
-            upper = block[:, :HALF, :].reshape(depth, orbitals)
-            lower = block[:, HALF:, :].reshape(depth, orbitals)
+            slot = lax.rem(step, DEPTH)
+            upper = blocks[slot, :, :HALF, :].reshape(depth, orbitals)
+            lower = blocks[slot, :, HALF:, :].reshape(depth, orbitals)
             total[...] += jnp.dot(
                 spread[chunk], jnp.concatenate([upper, lower], axis=1),
                 preferred_element_type=jnp.float32,
@@ -466,8 +508,8 @@
                recv_sem.at[across, step], target).wait()
 
 
-def step_kernel(count, sharers, electrons, theta_ref, half_ref, samples_ref, columns_ref,
-                vectors_ref, out_ref, half, theta, parts, arrived, coef, field, whole, spread,
+def step_kernel(count, sharers, electrons, columns_ref, inverse_ref, half_ref, samples_ref,
+                vectors_ref, out_ref, columns, matrices, grid, half, theta, parts, arrived, coef, field, whole, spread,
                 blocks, total, full, outgoing, incoming, finished, rows, half_sem, block_sem,
                 theta_send, theta_recv, part_send, part_recv, coef_send, coef_recv,
                 column_send, column_recv, walk_send, walk_recv, row_send, row_recv,
@@ -475,7 +517,7 @@
     me = position()
 
     def first_half(step, carry):
-        half_load(half_ref, half, half_sem, lax.rem(me + 1 + step, count)).start()
+        half_load(half_ref, half, half_sem, lax.rem((me // 2) * 2 + 2 + step, count)).start()
         return carry
 
     lax.fori_loop(0, count, first_half, 0)
@@ -485,12 +527,15 @@
         return carry
 
     lax.fori_loop(0, DEPTH - 1, first_blocks, 0)
-    greet([target for _, _, target in partners(count, sharers)])
-    bias_phase(count, sharers, theta_ref, half_ref, samples_ref, coef, half, theta, parts,
+    others = [target for _, _, target in partners(count, sharers)]
+    barrier = greet(others)
+    theta_phase(columns_ref, inverse_ref, theta, columns, matrices, grid)
+    pl.semaphore_wait(barrier, len(others))
+    bias_phase(count, sharers, half_ref, samples_ref, coef, half, theta, parts,
                arrived, half_sem, theta_send, theta_recv, part_send, part_recv, coef_send,
                coef_recv)
-    column_phase(count, columns_ref, whole, column_send, column_recv)
-    field_phase(count, sharers, coef, columns_ref, vectors_ref, field, whole, spread, blocks,
+    column_phase(count, columns, whole, column_send, column_recv)
+    field_phase(count, sharers, coef, columns, vectors_ref, field, whole, spread, blocks,
                 total, full, outgoing, incoming, finished, block_sem, column_send, column_recv,
                 walk_send, walk_recv, row_send, row_recv)
     walker_phase(count, sharers, electrons, field, whole, out_ref, out_send, out_recv, rows)
@@ -508,6 +553,7 @@
         count == local_walkers and row_block % ROWS == 0 and local_walkers % HALF == 0
         and width % LANES == 0 and LANES % VECTORS == 0 and width == LANES
         and electrons <= LANES and orbitals % LANES == 0
+        and flat % LANES == 0 and count % 2 == 0 and electrons % ROWS == 0
         and (row_block // ROWS) * (vectors // VECTORS) >= DEPTH
     )
     if not fits:
@@ -521,27 +567,19 @@
     dma = pltpu.SemaphoreType.DMA
     half_type, full_type = jnp.bfloat16, jnp.float32
     grid = walkers.reshape(local_walkers, 2, row_block, electrons)
-    pairs = jnp.concatenate([grid[:, 0], grid[:, 1]], axis=2)
-    inverse_real, inverse_imag = correlation_inverse[:, 0], correlation_inverse[:, 1]
-    theta = jnp.stack(
-        [
-            jnp.einsum("wmk,wkn->wmn", pairs, jnp.concatenate(side, axis=1),
-                       precision=lax.Precision.HIGH)
-            for side in ((inverse_real, -inverse_imag), (inverse_imag, inverse_real))
-        ],
-        0,
-    ).astype(half_type)
-    theta = theta.reshape(2 * local_walkers, flat)
-    columns = jnp.pad(grid.astype(half_type), ((0, 0), (0, 0), (0, 0), (0, LANES - electrons)))
+    columns = jnp.pad(grid, ((0, 0), (0, 0), (0, 0), (0, LANES - electrons)))
     columns = columns.transpose(0, 2, 1, 3).reshape(local_walkers, row_block, 2 * LANES)
     moved = pl.pallas_call(
         functools.partial(step_kernel, count, sharers, electrons),
         out_shape=jax.ShapeDtypeStruct((sharers * local_walkers, row_block, 2 * LANES), half_type),
         in_specs=[
-            pl.BlockSpec(memory_space=place) for place in (vmem, anywhere, vmem, vmem, anywhere)
+            pl.BlockSpec(memory_space=place) for place in (vmem, vmem, anywhere, vmem, anywhere)
         ],
         out_specs=pl.BlockSpec(memory_space=vmem),
         scratch_shapes=[
+            vmem((local_walkers, row_block, 2 * LANES), half_type),
+            vmem((2, 6 * LANES, 2 * LANES), half_type),
+            vmem((row_block, 2 * local_walkers, LANES), full_type),
             vmem((count, width, flat), half_type),
             vmem((sharers, 2 * local_walkers, flat), half_type),
             vmem((count, lines, width), full_type),
@@ -568,7 +606,7 @@
         compiler_params=pltpu.CompilerParams(
             collective_id=0, has_side_effects=True, vmem_limit_bytes=VMEM_LIMIT
         ),
-    )(theta, half_vectors, samples, columns, field_vectors)
+    )(columns, correlation_inverse, half_vectors, samples, field_vectors)
     chosen = jnp.take(moved, source, axis=0).reshape(local_walkers, row_block, 2, LANES)
     chosen = chosen[..., :electrons].transpose(0, 2, 1, 3)
     return chosen.reshape(local_walkers, 2, flat).astype(walkers.dtype)

time: 80 us -> 72 us (0.900)
  Pallas kernels: 70.5 us -> 66 us
  local copies, waits for them, and re-layouts: 6.69 us -> 5.44 us
  other arithmetic: 1.37 us -> 0.26 us
  matrix products: 1.07 us -> 0 us
    pallas_call x1, Pallas kernels: 70.5 us -> 66 us  [body(): pl.pallas_call(functools.partial(step_kernel, count, sharers, electrons),...]
    reshape x1 -> x2, local copies, waits for them, and re-layouts: 0.14 us -> 1.46 us  [body(): grid = walkers.reshape(local_walkers, 2, row_block, electrons)]
    squeeze x2 -> x0, local copies, waits for them, and re-layouts: 1.2 us -> none  [the longest x1 1.18 us: body(): correlation_inverse[:, 1]]
    dot_general x2 -> x0, matrix products: 1.07 us -> none  [body(): jnp.einsum('wmk,wkn->wmn', pairs, jnp.concatenate(side, axis=1), precisio...]
    unnamed x3 -> x2, local copies, waits for them, and re-layouts: 1.04 us -> 0.01 us
    neg x1 -> x0, other arithmetic: 1.03 us -> none  [body(): -inverse_imag]
    convert_element_type x1 -> x0, local copies, waits for them, and re-layouts: 0.86 us -> none  [body(): theta = jnp.stack([jnp.einsum('wmk,wkn->wmn', pairs, jnp.concatenate(side...]
where the time goes in v4:
time: 72 us; the launch traced here: 71.8 us
  Pallas kernels  66 us (92%)
  local copies, waits for them, and re-layouts  5.44 us (8%)
    pallas_call x1, Pallas kernels, body(): pl.pallas_call(functools.partial(step_kernel, count, sharers, electrons),...  66 us
    gather x2, local copies, waits for them, and re-layouts, body(): jnp.take(moved, source, axis=0).reshape(local_walkers, row_block, 2, LANES)  1.61 us
    reshape x2, local copies, waits for them, and re-layouts, body(): grid = walkers.reshape(local_walkers, 2, row_block, electrons)  1.46 us

profile of v4, /device:TPU:1, one launch (start us, length us, event | category | flops | bytes accessed | tf_op | source)
XLA Modules:
  0.0 71.8 jit_solution(235498835975324120)
XLA Ops:
  0.0 0.0 copy-start
  0.0 1.3 %reshape.16 = f32[8,2,48,96]{3,2,1,0:T(8,128)S(1)} reshape(f32[8,2,4608]{2,1,0:T(2,128)} %param.6) | data formatting | bytes 589824 | tf_op jit(solution)/shard_map/reshape | solution.py:569
  1.3 0.2 copy.7
  1.5 0.2 pad_bitcast_fusion
  1.7 1.0 %reshape.17.columns_ref = f32[8,48,256]{2,1,0:T(8,128)} reshape(f32[8,48,2,128]{3,2,1,0:T(2,128)S(1)} %pad_bitcast_fusion) | data formatting | bytes 786432 | tf_op jit(solution)/shard_map/reshape | solution.py:571
  2.7 66.0 %shard_map.64 = bf16[16,48,256]{2,1,0:T(8,128)(2,1)} custom-call(f32[8,48,256]{2,1,0:T(8,128)} %reshape.17.columns_ref, f32[8,2,96,96]{3,2,1,0:T(8,128)} %inverse_ref.1, bf16[1024,4608]{1,0:T(8,128)(2,1)} %half_ref.1, f32[16,1024]{1,0:T(8,128)} %samples_ref.1, bf16[1024,48,384]{2,1,0:T(8,128)(2,1)} %vectors_ref.1), custom_call_target="tpu_custom_call" | custom-call | tf_op jit(solution)/shard_map/pallas_call | solution.py:572
  68.8 0.0 copy-done
  68.8 1.6 %gather_fusion = bf16[8,48,256]{2,1,0:T(8,128)(2,1)S(1)} fusion(bf16[16,48,256]{2,1,0:T(8,128)(2,1)} %shard_map.64, s32[1024]{0:T(1024)S(1)} %pad_clamp_fusion), kind=kCustom, calls=%fused_computation | custom fusion | bytes 393248 | tf_op jit(solution)/shard_map/jit(_take)/gather | solution.py:610
  70.4 0.1 gather.7
  70.5 0.2 convert_bitcast_fusion
  70.7 1.1 %reshape.18 = f32[8,2,4608]{2,1,0:T(2,128)} reshape(f32[8,2,48,96]{3,2,1,0:T(8,128)S(1)} %copy.8) | data formatting | bytes 589824 | tf_op jit(solution)/shard_map/convert_element_type | solution.py:612
  (4 shorter events, 0.0 us)
Async XLA Ops:
  0.0 68.8 %copy-start = (s32[8]{0:T(128)S(1)}, s32[8]{0:T(128)}, u32[]{:S(2)}) copy-start(s32[8]{0:T(128)} %param.11) | copy-start | bytes 100

commit v5 on v4

--- a/solution.py
+++ b/solution.py
@@ -175,10 +175,35 @@
     )
 
 
-def theta_phase(columns_ref, inverse_ref, theta, columns, matrices, grid):
+def to_rows(flat_ref, grid, electrons):
+    lane = lax.broadcasted_iota(jnp.int32, (flat_ref.shape[0], LANES), 1)
+    for row in range(grid.shape[0]):
+        start, shift = row * electrons // LANES * LANES, row * electrons % LANES
+        back = (LANES - shift) % LANES
+        value = pltpu.roll(flat_ref[:, start:start + LANES], back, 1)
+        if shift + electrons > LANES:
+            after = pltpu.roll(flat_ref[:, start + LANES:start + 2 * LANES], back, 1)
+            value = jnp.where(lane < LANES - shift, value, after)
+        grid[row] = jnp.where(lane < electrons, value, 0.0)
+
+
+def to_flat(grid, electrons):
+    lane = lax.broadcasted_iota(jnp.int32, (grid.shape[1], LANES), 1)
+    for tile in range(grid.shape[0] * electrons // LANES):
+        start = tile * LANES
+        value = None
+        for row in range(start // electrons, (start + LANES - 1) // electrons + 1):
+            moved = pltpu.roll(grid[row], row * electrons % LANES, 1)
+            value = moved if value is None else jnp.where(
+                lane < row * electrons - start, value, moved)
+        yield start, value
+
+
+def theta_phase(walkers_ref, inverse_ref, theta, columns, matrices, rows_in, grid):
     walk = lax.axis_index("walk")
-    local, row_block = columns_ref.shape[0], columns_ref.shape[1]
+    local = inverse_ref.shape[0]
     electrons = inverse_ref.shape[2]
+    to_rows(walkers_ref, rows_in, electrons)
     size = 2 * LANES
     matrices[...] = jnp.zeros_like(matrices)
     for walker in range(local):
@@ -191,20 +216,14 @@
             matrix[first:first + electrons, LANES:LANES + electrons] = imag_parts[part]
             matrix[second:second + electrons, :electrons] = -imag_parts[part]
             matrix[second:second + electrons, LANES:LANES + electrons] = real_parts[part]
-        high, low = two_parts(columns_ref[walker])
+        pair = [rows_in[:, 2 * walker + side, :] for side in range(2)]
+        high, low = two_parts(jnp.concatenate(pair, axis=1))
         columns[walker] = high
         rotated = jnp.dot(jnp.concatenate([high, low, high], axis=1), matrix[...],
                           preferred_element_type=jnp.float32)
         grid[:, walker, :] = rotated[:, :LANES]
         grid[:, local + walker, :] = rotated[:, LANES:]
-    lane = lax.broadcasted_iota(jnp.int32, (2 * local, LANES), 1)
-    for tile in range(row_block * electrons // LANES):
-        start = tile * LANES
-        value = None
-        for row in range(start // electrons, (start + LANES - 1) // electrons + 1):
-            moved = pltpu.roll(grid[row], row * electrons % LANES, 1)
-            value = moved if value is None else jnp.where(
-                lane < row * electrons - start, value, moved)
+    for start, value in to_flat(grid, electrons):
         theta[walk, :, start:start + LANES] = value.astype(jnp.bfloat16)
 
 
@@ -337,7 +356,6 @@
     chunks = vectors_ref.shape[0] // VECTORS
     groups = row_block // ROWS
     lines = coef_ref.shape[1]
-    per_block = coef_ref.shape[2] // VECTORS
     depth = VECTORS * HALF
 
     def load(step):
@@ -349,18 +367,14 @@
     row_place = lax.broadcasted_iota(jnp.int32, (HALF, depth), 1)
     diagonal = (lax.rem(row_place, HALF) == row_at).astype(jnp.float32)
 
-    for part in range(per_block):
-        picks = (vector_at == place // HALF + part * VECTORS).astype(jnp.bfloat16)
-
-        def widen(block, carry):
-            repeated = jnp.dot(coef_ref[block], picks, preferred_element_type=jnp.float32)
-            wide = repeated[:, None, :] * diagonal[None]
-            spread[block * per_block + part] = wide.reshape(lines * HALF, depth).astype(
-                jnp.bfloat16
-            )
-            return carry
-
-        lax.fori_loop(0, coef_ref.shape[0], widen, 0)
+    picks = (vector_at == place // HALF).astype(jnp.bfloat16)
+
+    def widen(block):
+        repeated = jnp.dot(coef_ref[block], picks, preferred_element_type=jnp.float32)
+        wide = repeated[:, None, :] * diagonal[None]
+        spread[block] = wide.reshape(lines * HALF, depth).astype(jnp.bfloat16)
+
+    widen(0)
 
     def walk_copy(group, step, arriving):
         other = lax.rem(walk + step, sharers) if not arriving else lax.rem(
@@ -410,6 +424,8 @@
                 spread[chunk], jnp.concatenate([upper, lower], axis=1),
                 preferred_element_type=jnp.float32,
             )
+            if group == 0:
+                widen(jnp.minimum(chunk + 1, chunks - 1))
             return carry
 
         lax.fori_loop(0, chunks, add, 0)
@@ -455,8 +471,8 @@
     )
 
 
-def walker_phase(count, sharers, electrons, field_ref, whole_ref, out_ref,
-                 send_sem, recv_sem, rows):
+def walker_phase(count, sharers, electrons, field_ref, whole_ref, source_ref, out_ref,
+                 moved, grid, send_sem, recv_sem, rows):
     me, walk = position(), lax.axis_index("walk")
     row_block = rows.shape[1]
     orbitals = field_ref.shape[1]
@@ -497,19 +513,25 @@
     mine = walk * count + me
     for across, step, target in others:
         index = lax.rem(me + step, count)
-        remote(rows.at[index], out_ref.at[mine], send_sem.at[across, step],
+        remote(rows.at[index], moved.at[mine], send_sem.at[across, step],
                recv_sem.at[across, step], target).start()
-    out_ref[mine] = rows[me]
+    moved[mine] = rows[me]
     for across, step, target in others:
         index = lax.rem(me + step, count)
         giver = lax.rem(walk + sharers - across, sharers) * count + lax.rem(
             me + count - step, count)
-        remote(rows.at[index], out_ref.at[giver], send_sem.at[across, step],
+        remote(rows.at[index], moved.at[giver], send_sem.at[across, step],
                recv_sem.at[across, step], target).wait()
-
-
-def step_kernel(count, sharers, electrons, columns_ref, inverse_ref, half_ref, samples_ref,
-                vectors_ref, out_ref, columns, matrices, grid, half, theta, parts, arrived, coef, field, whole, spread,
+    for walker in range(count):
+        taken = moved[source_ref[walker]].astype(jnp.float32)
+        for side in range(2):
+            grid[:, 2 * walker + side, :] = taken[:, side * LANES:(side + 1) * LANES]
+    for start, value in to_flat(grid, electrons):
+        out_ref[:, start:start + LANES] = value
+
+
+def step_kernel(count, sharers, electrons, walkers_ref, inverse_ref, half_ref, samples_ref, source_ref,
+                vectors_ref, out_ref, moved, columns, matrices, rows_in, grid, half, theta, parts, arrived, coef, field, whole, spread,
                 blocks, total, full, outgoing, incoming, finished, rows, half_sem, block_sem,
                 theta_send, theta_recv, part_send, part_recv, coef_send, coef_recv,
                 column_send, column_recv, walk_send, walk_recv, row_send, row_recv,
@@ -529,7 +551,7 @@
     lax.fori_loop(0, DEPTH - 1, first_blocks, 0)
     others = [target for _, _, target in partners(count, sharers)]
     barrier = greet(others)
-    theta_phase(columns_ref, inverse_ref, theta, columns, matrices, grid)
+    theta_phase(walkers_ref, inverse_ref, theta, columns, matrices, rows_in, grid)
     pl.semaphore_wait(barrier, len(others))
     bias_phase(count, sharers, half_ref, samples_ref, coef, half, theta, parts,
                arrived, half_sem, theta_send, theta_recv, part_send, part_recv, coef_send,
@@ -538,7 +560,8 @@
     field_phase(count, sharers, coef, columns, vectors_ref, field, whole, spread, blocks,
                 total, full, outgoing, incoming, finished, block_sem, column_send, column_recv,
                 walk_send, walk_recv, row_send, row_recv)
-    walker_phase(count, sharers, electrons, field, whole, out_ref, out_send, out_recv, rows)
+    walker_phase(count, sharers, electrons, field, whole, source_ref, out_ref, moved, grid,
+                 out_send, out_recv, rows)
 
 
 def body(walkers, correlation_inverse, half_vectors, field_vectors, samples, source):
@@ -551,7 +574,7 @@
     width = vectors // count
     fits = (
         count == local_walkers and row_block % ROWS == 0 and local_walkers % HALF == 0
-        and width % LANES == 0 and LANES % VECTORS == 0 and width == LANES
+        and width % LANES == 0 and width == LANES == VECTORS
         and electrons <= LANES and orbitals % LANES == 0
         and flat % LANES == 0 and count % 2 == 0 and electrons % ROWS == 0
         and (row_block // ROWS) * (vectors // VECTORS) >= DEPTH
@@ -566,19 +589,18 @@
     vmem, anywhere = pltpu.VMEM, pl.ANY
     dma = pltpu.SemaphoreType.DMA
     half_type, full_type = jnp.bfloat16, jnp.float32
-    grid = walkers.reshape(local_walkers, 2, row_block, electrons)
-    columns = jnp.pad(grid, ((0, 0), (0, 0), (0, 0), (0, LANES - electrons)))
-    columns = columns.transpose(0, 2, 1, 3).reshape(local_walkers, row_block, 2 * LANES)
-    moved = pl.pallas_call(
+    result = pl.pallas_call(
         functools.partial(step_kernel, count, sharers, electrons),
-        out_shape=jax.ShapeDtypeStruct((sharers * local_walkers, row_block, 2 * LANES), half_type),
+        out_shape=jax.ShapeDtypeStruct((2 * local_walkers, flat), walkers.dtype),
         in_specs=[
-            pl.BlockSpec(memory_space=place) for place in (vmem, vmem, anywhere, vmem, anywhere)
+            pl.BlockSpec(memory_space=place) for place in (vmem, vmem, anywhere, vmem, pltpu.SMEM, anywhere)
         ],
         out_specs=pl.BlockSpec(memory_space=vmem),
         scratch_shapes=[
+            vmem((sharers * local_walkers, row_block, 2 * LANES), half_type),
             vmem((local_walkers, row_block, 2 * LANES), half_type),
             vmem((2, 6 * LANES, 2 * LANES), half_type),
+            vmem((row_block, 2 * local_walkers, LANES), full_type),
             vmem((row_block, 2 * local_walkers, LANES), full_type),
             vmem((count, width, flat), half_type),
             vmem((sharers, 2 * local_walkers, flat), half_type),
@@ -606,10 +628,9 @@
         compiler_params=pltpu.CompilerParams(
             collective_id=0, has_side_effects=True, vmem_limit_bytes=VMEM_LIMIT
         ),
-    )(columns, correlation_inverse, half_vectors, samples, field_vectors)
-    chosen = jnp.take(moved, source, axis=0).reshape(local_walkers, row_block, 2, LANES)
-    chosen = chosen[..., :electrons].transpose(0, 2, 1, 3)
-    return chosen.reshape(local_walkers, 2, flat).astype(walkers.dtype)
+    )(walkers.reshape(2 * local_walkers, flat), correlation_inverse, half_vectors, samples, source,
+      field_vectors)
+    return result.reshape(walkers.shape)
 
 
 def solution(mesh):

time: 72 us -> 69.7 us (0.968)
  local copies, waits for them, and re-layouts: 5.44 us -> 3.72 us
    gather x2 -> x0, local copies, waits for them, and re-layouts: 1.61 us -> none  [body(): jnp.take(moved, source, axis=0).reshape(local_walkers, row_block, 2, LANES)]
    reshape x3 -> x2, local copies, waits for them, and re-layouts: 2.51 us -> 3.72 us  [the longest x1 1.88 us: body(): walkers.reshape(2 * local_walkers, flat)]
    convert_element_type x2 -> x0, local copies, waits for them, and re-layouts: 1.12 us -> none  [body(): return chosen.reshape(local_walkers, 2, flat).astype(walkers.dtype)]
where the time goes in v5:
time: 69.7 us; the launch traced here: 69.5 us
  Pallas kernels  65.7 us (94%)
  local copies, waits for them, and re-layouts  3.72 us (5%)
    pallas_call x1, Pallas kernels, body(): pl.pallas_call(functools.partial(step_kernel, count, sharers, electrons),...  65.7 us
    reshape x1, local copies, waits for them, and re-layouts, body(): walkers.reshape(2 * local_walkers, flat)  1.88 us
    reshape x1, local copies, waits for them, and re-layouts, body(): return result.reshape(walkers.shape)  1.84 us

profile of v5, /device:TPU:1, one launch (start us, length us, event | category | flops | bytes accessed | tf_op | source)
XLA Modules:
  0.0 69.5 jit_solution(3831395279391056090)
XLA Ops:
  0.0 1.9 %reshape.6.walkers_ref = f32[16,4608]{1,0:T(8,128)} reshape(f32[8,2,4608]{2,1,0:T(2,128)} %param.6) | data formatting | bytes 589824 | tf_op jit(solution)/shard_map/reshape | solution.py:631
  1.9 65.7 %shard_map.64 = f32[16,4608]{1,0:T(8,128)} custom-call(f32[16,4608]{1,0:T(8,128)} %reshape.6.walkers_ref, f32[8,2,96,96]{3,2,1,0:T(8,128)} %inverse_ref.1, bf16[1024,4608]{1,0:T(8,128)(2,1)} %half_ref.1, f32[16,1024]{1,0:T(8,128)} %samples_ref.1, s32[8]{0:T(128)} %source_ref.1, bf16[1024,48,384]{2,1,0:T(8,128)(2,1)} %vectors_ref.1), custom_call_target="tpu_custom_call" | custom-call | tf_op jit(solution)/shard_map/pallas_call | solution.py:592
  67.6 1.8 %reshape.7 = f32[8,2,4608]{2,1,0:T(2,128)} reshape(f32[16,4608]{1,0:T(8,128)} %shard_map.64) | data formatting | bytes 589824 | tf_op jit(solution)/shard_map/reshape | solution.py:633

commit v6 on v5

--- a/solution.py
+++ b/solution.py
@@ -176,13 +176,17 @@
 
 
 def to_rows(flat_ref, grid, electrons):
-    lane = lax.broadcasted_iota(jnp.int32, (flat_ref.shape[0], LANES), 1)
+    lane = lax.broadcasted_iota(jnp.int32, (grid.shape[1], LANES), 1)
+
+    def tile_at(start):
+        return flat_ref[:, :, start:start + LANES].reshape(grid.shape[1], LANES)
+
     for row in range(grid.shape[0]):
         start, shift = row * electrons // LANES * LANES, row * electrons % LANES
         back = (LANES - shift) % LANES
-        value = pltpu.roll(flat_ref[:, start:start + LANES], back, 1)
+        value = pltpu.roll(tile_at(start), back, 1)
         if shift + electrons > LANES:
-            after = pltpu.roll(flat_ref[:, start + LANES:start + 2 * LANES], back, 1)
+            after = pltpu.roll(tile_at(start + LANES), back, 1)
             value = jnp.where(lane < LANES - shift, value, after)
         grid[row] = jnp.where(lane < electrons, value, 0.0)
 
@@ -527,7 +531,7 @@
         for side in range(2):
             grid[:, 2 * walker + side, :] = taken[:, side * LANES:(side + 1) * LANES]
     for start, value in to_flat(grid, electrons):
-        out_ref[:, start:start + LANES] = value
+        out_ref[:, :, start:start + LANES] = value.reshape(count, 2, LANES)
 
 
 def step_kernel(count, sharers, electrons, walkers_ref, inverse_ref, half_ref, samples_ref, source_ref,
@@ -591,7 +595,7 @@
     half_type, full_type = jnp.bfloat16, jnp.float32
     result = pl.pallas_call(
         functools.partial(step_kernel, count, sharers, electrons),
-        out_shape=jax.ShapeDtypeStruct((2 * local_walkers, flat), walkers.dtype),
+        out_shape=jax.ShapeDtypeStruct(walkers.shape, walkers.dtype),
         in_specs=[
             pl.BlockSpec(memory_space=place) for place in (vmem, vmem, anywhere, vmem, pltpu.SMEM, anywhere)
         ],
@@ -628,9 +632,9 @@
         compiler_params=pltpu.CompilerParams(
             collective_id=0, has_side_effects=True, vmem_limit_bytes=VMEM_LIMIT
         ),
-    )(walkers.reshape(2 * local_walkers, flat), correlation_inverse, half_vectors, samples, source,
+    )(walkers, correlation_inverse, half_vectors, samples, source,
       field_vectors)
-    return result.reshape(walkers.shape)
+    return result
 
 
 def solution(mesh):

time: 69.7 us -> 67.7 us (0.971)
  local copies, waits for them, and re-layouts: 3.72 us -> 1.69 us
    reshape x2 -> x0, local copies, waits for them, and re-layouts: 3.72 us -> none  [the longest x1 1.88 us: body(): walkers.reshape(2 * local_walkers, flat)]
    unnamed x0 -> x1, local copies, waits for them, and re-layouts: none -> 1.69 us
where the time goes in v6:
time: 67.7 us; the launch traced here: 67.5 us
  Pallas kernels  65.8 us (97%)
  local copies, waits for them, and re-layouts  1.69 us (2%)
    pallas_call x1, Pallas kernels, body(): pl.pallas_call(functools.partial(step_kernel, count, sharers, electrons),...  65.8 us
    unnamed x1, local copies, waits for them, and re-layouts  1.69 us

profile of v6, /device:TPU:1, one launch (start us, length us, event | category | flops | bytes accessed | tf_op | source)
XLA Modules:
  0.0 67.5 jit_solution(6540725903628435565)
XLA Ops:
  0.0 65.8 %shard_map.64 = f32[8,2,4608]{2,1,0:T(2,128)} custom-call(f32[8,2,4608]{2,1,0:T(2,128)} %walkers_ref.1, f32[8,2,96,96]{3,2,1,0:T(8,128)} %inverse_ref.1, bf16[1024,4608]{1,0:T(8,128)(2,1)} %half_ref.1, f32[16,1024]{1,0:T(8,128)} %samples_ref.1, s32[8]{0:T(128)} %source_ref.1, bf16[1024,48,384]{2,1,0:T(8,128)(2,1)} %vectors_ref.1), custom_call_target="tpu_custom_call" | custom-call | tf_op jit(solution)/shard_map/pallas_call | solution.py:596
  65.8 1.7 %copy.8 = f32[8,2,4608]{2,1,0:T(2,128)} copy(f32[8,2,4608]{2,1,0:T(2,128)} %shard_map.64) | data formatting | bytes 589824
